TPU v7x, 32 devices: a whole 2x2x4 slice. The times are simulated.
32 devices in a mesh: dp: 16 (over z, x, core), mp: 2 (over y).
Axes of the slice: x: 2, y: 2, z: 4, core: 2. Of those that a mesh axis runs over, the one named last changes fastest.
Arguments:
- layer_input: float32 [4096, 512], P('dp'), may hold values from -6 to 6
- grad_out: float32 [4096, 512], P('dp'), may hold values from -6 to 6
- segment: int32 [16, 256], P('dp'), may hold values from 0 to 7, never falling along the last dimension, each value on 1 to 128 neighbouring positions
- item_ids: int32 [4096], P('dp'), may hold values from 0 to 31
- w_uvqk: float32 [512, 2048], P(None, 'mp'), may hold values from -0.25 to 0.25
- w_out: float32 [512, 512], P('mp'), may hold values from -0.25 to 0.25
- table: float32 [32, 512], P(('dp', 'mp')), may hold values from -6 to 6
- accum: float32 [32], P(('dp', 'mp')), may hold values from 0.1 to 2
Outputs:
- w_uvqk_grad: float32 [512, 2048], P(None, 'mp')
- w_out_grad: float32 [512, 512], P('mp')
- new_table: float32 [32, 512], P(('dp', 'mp'))
- new_accum: float32 [32], P(('dp', 'mp'))
Inputs may be any that keep to these rules, and one draw needn't show every extreme that they name: `segment`: segment numbers never fall along a row; a history holds at most 128 tokens and some history holds exactly that many.
All inputs are finite; a program needn't handle non-finite values.
Results may differ from a plain program's by a relative error of at most 0.0003.
Values sent between devices are 32-bit elements; how exact they have to be, the bound alone decides.
A program may use at most 64 MiB of HBM per device.

v0:
```python
import jax
import jax.numpy as jnp
from jax import lax
from jax.sharding import PartitionSpec as P

HEAD_DIM = 64


highest = lax.Precision.HIGHEST


def mdot(left, right):
    return jnp.dot(left, right, precision=highest, preferred_element_type=jnp.float32)


def onehot_sum(item_ids, targets, values):
    table_hits = (item_ids[:, None] == targets[None, :]).astype(jnp.float32)
    return lax.dot_general(
        table_hits,
        values,
        (((0,), (0,)), ((), ())),
        precision=highest,
        preferred_element_type=jnp.float32,
    )


def body(layer_input, grad_out, segment, item_ids, w_uvqk, w_out, table, accum):
    count = layer_input.shape[0]
    width = layer_input.shape[1]
    local = w_uvqk.shape[1] // (4 * HEAD_DIM)
    scale = HEAD_DIM ** (-0.5)
    pre = mdot(layer_input, w_uvqk).reshape(count, local, 4, HEAD_DIM)
    act = jax.nn.silu(pre)
    ublk, vblk, qblk, kblk = (act[:, :, 0], act[:, :, 1], act[:, :, 2], act[:, :, 3])
    seg_row = segment[0]
    place = jnp.arange(count)
    mask = ((seg_row[:, None] == seg_row[None, :]) & (place[:, None] >= place[None, :])).astype(
        jnp.float32
    )
    score = jnp.einsum("ihd,jhd->hij", qblk, kblk, precision=highest) * scale
    sigm = jax.nn.sigmoid(score)
    attn = score * sigm * mask
    outv = jnp.einsum("hij,jhd->ihd", attn, vblk, precision=highest).reshape(
        count, local * HEAD_DIM
    )
    sums = lax.psum((jnp.sum(outv, axis=1), jnp.sum(outv * outv, axis=1)), "mp")
    mean = sums[0][:, None] / width
    var = sums[1][:, None] / width - mean * mean
    rstd = lax.rsqrt(var + 1e-05)
    normed = (outv - mean) * rstd
    nheads = normed.reshape(count, local, HEAD_DIM)
    zval = (nheads * ublk).reshape(count, local * HEAD_DIM)
    dzval = mdot(grad_out, w_out.T).reshape(count, local, HEAD_DIM)
    w_out_part = mdot(zval.T, grad_out)
    dnorm = (dzval * ublk).reshape(count, local * HEAD_DIM)
    dublk = dzval * nheads
    grads_sum = lax.psum((jnp.sum(dnorm, axis=1), jnp.sum(dnorm * normed, axis=1)), "mp")
    first = grads_sum[0][:, None] / width
    second = grads_sum[1][:, None] / width
    dout = (rstd * (dnorm - first - normed * second)).reshape(count, local, HEAD_DIM)
    dattn = jnp.einsum("ihd,jhd->hij", dout, vblk, precision=highest)
    dvblk = jnp.einsum("hij,ihd->jhd", attn, dout, precision=highest)
    dscore = dattn * mask * (sigm * (1.0 + score * (1.0 - sigm))) * scale
    dqblk = jnp.einsum("hij,jhd->ihd", dscore, kblk, precision=highest)
    dkblk = jnp.einsum("hij,ihd->jhd", dscore, qblk, precision=highest)
    dact = jnp.stack([dublk, dvblk, dqblk, dkblk], axis=2)
    psig = jax.nn.sigmoid(pre)
    dpre = (dact * psig * (1.0 + pre * (1.0 - psig))).reshape(count, local * 4 * HEAD_DIM)
    w_uvqk_part = mdot(layer_input.T, dpre)
    w_uvqk_grad, w_out_grad = lax.psum((w_uvqk_part, w_out_part), "dp")
    head_part = mdot(dpre, w_uvqk.T)
    own_rows = table.shape[0]
    n_dp = lax.axis_size("dp")
    n_mp = lax.axis_size("mp")
    cols = width // n_mp
    own_cols = lax.dynamic_slice_in_dim(grad_out, lax.axis_index("mp") * cols, cols, 1)
    x_cols = lax.psum_scatter(head_part, "mp", scatter_dimension=1, tiled=True) + own_cols
    targets = jnp.arange(own_rows * n_dp * n_mp, dtype=jnp.int32)
    slab = onehot_sum(item_ids, targets, x_cols)
    group_rows = lax.psum_scatter(slab, "dp", scatter_dimension=0, tiled=True)
    row_grad = lax.all_to_all(group_rows, "mp", split_axis=0, concat_axis=1, tiled=True)
    new_accum = accum + jnp.sum(row_grad * row_grad, axis=1) / width
    new_table = table - 0.5 * row_grad * lax.rsqrt(new_accum)[:, None]
    return (w_uvqk_grad, w_out_grad, new_table, new_accum)


def solution(mesh):
    placed = (
        P("dp", None),
        P("dp", None),
        P("dp", None),
        P("dp"),
        P(None, "mp"),
        P("mp", None),
        P(("dp", "mp"), None),
        P(("dp", "mp")),
    )
    return jax.shard_map(
        body,
        mesh=mesh,
        in_specs=placed,
        out_specs=(P(None, "mp"), P("mp", None), P(("dp", "mp"), None), P(("dp", "mp"))),
        check_vma=False,
    )
```

profile of v0, /device:TPU:0, one launch (start us, length us, event | category | flops | bytes accessed | tf_op | source)
XLA Modules:
  0.0 170.5 jit_solution(18024275651644727226)
XLA Ops:
  8.0 0.0 copy-start
  8.0 0.0 reduce-scatter.2.cloned.1.call-start
  8.1 1.5 copy-done
  9.6 2.9 %fusion.15 = f32[256,1024]{1,0:T(8,128)S(1)} fusion(f32[256,512]{1,0:T(8,128)} %param.8, f32[512,1024]{1,0:T(8,128)S(1)} %copy-done), kind=kOutput, calls=%fused_computation.46 | convolution fusion | flops 1610612736 | bytes 3670016 | tf_op jit(solution)/shard_map/dot_general | solution.py:13
  12.5 0.0 copy-start.1
  12.5 1.3 copy.22
  13.9 0.0 copy-done.1
  13.9 1.5 divide_multiply_fusion
  15.4 0.7 slice.19
  16.1 1.1 convolution_multiply_fusion.1
  17.2 0.0 copy-start.6
  17.2 0.0 copy-done.11
  17.2 0.1 fusion.9
  17.3 1.3 fusion.4
  18.7 5.9 %all-reduce.3 = (f32[256]{0:T(256)S(1)}, f32[256]{0:T(256)S(1)}) all-reduce(f32[256]{0:T(256)S(1)} %get-tuple-element.28, f32[256]{0:T(256)S(1)} %reduce_sum.45), channel_id=1, replica_groups=mesh['dp'=16,'mp'=2] {'mp'}, use_global_device_ids=true, to_apply=%region_3.4 | all-reduce | flops 512 | bytes 4096 | tf_op jit(solution)/shard_map/psum | solution.py:46
  24.6 2.6 %fusion.13 = (f32[256]{0:T(256)S(1)}, f32[256]{0:T(256)S(1)}, f32[256,256]{0,1:T(8,128)}) fusion(f32[256,4,1,64]{0,3,1,2:T(8,128)} %slice.19, f32[256]{0:T(256)S(1)} %get-tuple-element.27, f32[256]{0:T(256)S(1)} %get-tuple-element.26, f32[4,64,256]{2,1,0:T(8,128)S(1)} %get-tuple-element.29, f32[256,512]{1,0:T(8,128)} %param.9, f32[256,512]{1,0:T(8,128)} %param.13), kind=kOutput, calls=%fused_computation.44 | convolution fusion | flops 403045888 | bytes 1839104 | tf_op jit(solution)/shard_map/dot_general | solution.py:13
  27.2 5.1 %all-reduce.2 = (f32[256]{0:T(256)S(1)}, f32[256]{0:T(256)S(1)}) all-reduce(f32[256]{0:T(256)S(1)} %get-tuple-element.17, f32[256]{0:T(256)S(1)} %get-tuple-element.16), channel_id=1, replica_groups=mesh['dp'=16,'mp'=2] {'mp'}, use_global_device_ids=true, to_apply=%region_7.8 | all-reduce | flops 512 | bytes 4096 | tf_op jit(solution)/shard_map/psum | solution.py:57
  32.3 1.1 subtract_multiply_fusion
  33.4 2.4 %convolution_bitcast_fusion.3 = f32[256,4,1,64]{0,3,1,2:T(8,128)S(1)} fusion(f32[256,4,64]{0,2,1:T(8,128)S(1)} %bitcast.88, f32[4,256,256]{2,1,0:T(8,128)} %copy-done.6, f32[256,256]{1,0:T(8,128)} %copy-done.9), kind=kOutput, calls=%fused_computation.7 | convolution fusion | flops 202637312 | bytes 1835008 | tf_op jit(solution)/shard_map/hij,ihd->jhd/dot_general | solution.py:62
  35.8 1.3 fusion.1
  37.2 0.0 copy-start.4
  37.2 0.8 convolution_bitcast_fusion.1
  38.0 1.1 convolution_bitcast_fusion.2
  39.1 0.0 copy-done.4
  39.1 0.8 bitcast_multiply_fusion
  39.8 0.1 pad_maximum_fusion
  39.9 0.0 copy-start.2
  40.0 1.1 copy.25
  41.1 2.5 %copy.26 = f32[256,1024]{1,0:T(8,128)} copy(f32[256,1024]{0,1:T(8,128)} %bitcast.84) | data formatting | bytes 2097152 | tf_op jit(solution)/shard_map/stack | solution.py:66
  43.6 4.3 %fusion.14 = f32[256,512]{1,0:T(8,128)} fusion(f32[512,1024]{1,0:T(8,128)S(1)} %copy-done, f32[256,1024]{1,0:T(8,128)S(1)} %copy-done.2, f32[256,1024]{1,0:T(8,128)} %copy.26), kind=kOutput, calls=%fused_computation.45 | convolution fusion | flops 1612709888 | bytes 4718592 | tf_op jit(solution)/shard_map/dot_general | solution.py:13
  47.9 0.0 reduce-scatter.2.cloned.1.call-update
  47.9 0.0 all-reduce.6.cloned.1.call-start
  48.0 2.5 %fusion.16 = f32[256,512]{1,0:T(8,128)} fusion(f32[256,256]{0,1:T(8,128)S(1)} %bitcast.87, f32[256,512]{1,0:T(8,128)} %param.9), kind=kOutput, calls=%fused_computation.47 | convolution fusion | flops 402653184 | bytes 1310720 | tf_op jit(solution)/shard_map/dot_general | solution.py:13
  50.5 4.8 %convolution_bitcast_fusion = f32[512,1024]{0,1:T(8,128)} fusion(f32[256,512]{1,0:T(8,128)} %param.8, f32[256,1024]{1,0:T(8,128)S(1)} %copy-done.2, f32[256,1024]{1,0:T(8,128)} %copy.26), kind=kOutput, calls=%fused_computation | convolution fusion | flops 1612709888 | bytes 4718592 | tf_op jit(solution)/shard_map/dot_general | solution.py:13
  55.3 0.0 all-reduce.6.cloned.1.call-update
  55.3 0.6 copy-done.14
  55.9 0.6 dynamic-slice
  57.2 7.2 %reduce-scatter.2.cloned.1.call-done = f32[256,256]{1,0:T(8,128)} async-done(((f32[256,512]{1,0:T(8,128)}), f32[256,256]{1,0:T(8,128)}) %reduce-scatter.2.cloned.1.call-update) | async-done | bytes 262160 | tf_op jit(solution)/shard_map/reduce_scatter | solution.py:77
  64.4 1.3 fusion.5
  65.7 61.7 %all-reduce = f32[32,256]{1,0:T(8,128)S(1)} all-reduce(f32[32,256]{1,0:T(8,128)S(1)} %fusion.5), channel_id=3, replica_groups=mesh['dp'=16,'mp'=2] {'dp'}, use_global_device_ids=true, to_apply=%region_11.12.clone | all-reduce | flops 8192 | bytes 65536
  127.4 0.6 copy.27
  128.0 3.2 %all-to-all-start = ((f32[2,1,256]{2,1,0:T(1,128)}), f32[2,1,256]{2,1,0:T(1,128)S(1)}, u32[]{:S(2)}, u32[]{:S(2)}) async-start(f32[2,1,256]{2,1,0:T(1,128)} %copy.27), calls=%async_computation.1 | async-start | bytes 4096 | tf_op jit(solution)/shard_map/all_to_all | solution.py:81
  131.9 3.1 %all-to-all-done = f32[2,1,256]{2,1,0:T(1,128)S(1)} async-done(((f32[2,1,256]{2,1,0:T(1,128)}), f32[2,1,256]{2,1,0:T(1,128)S(1)}, u32[]{:S(2)}, u32[]{:S(2)}) %all-to-all-start) | async-done | bytes 2080 | tf_op jit(solution)/shard_map/all_to_all | solution.py:81
  135.0 0.6 multiply_reduce_fusion.1
  136.3 0.6 sub.48
  136.9 21.2 %all-reduce.6.cloned.1.call-done = (f32[512,1024]{0,1:T(8,128)}, f32[256,512]{1,0:T(8,128)}) async-done(((f32[512,1024]{0,1:T(8,128)}, f32[256,512]{1,0:T(8,128)}), (f32[512,1024]{0,1:T(8,128)}, f32[256,512]{1,0:T(8,128)})) %all-reduce.6.cloned.1.call-update) | async-done | bytes 2621456 | tf_op jit(solution)/shard_map/psum | solution.py:70
  158.2 2.9 %copy.28 = f32[512,1024]{1,0:T(8,128)} copy(f32[512,1024]{0,1:T(8,128)} %get-tuple-element.18) | data formatting | bytes 4194304
  161.1 0.8 copy.33
  (25 shorter events, 0.1 us)
Async XLA Ops:
  8.0 1.6 copy-start
  8.0 56.4 %reduce-scatter.2.cloned.1.call-start = ((), (), s32[]{:S(2)}) async-start(), calls=%async_computation.2 | async-start | bytes 786432 | tf_op jit(solution)/shard_map/reduce_scatter | solution.py:77
  12.5 1.3 copy-start.1
  13.9 3.3 %copy-start.11 = (s32[1,256]{1,0:T(1,128)S(1)}, s32[1,256]{1,0:T(1,128)}, u32[]{:S(2)}) copy-start(s32[1,256]{1,0:T(1,128)} %param.10) | copy-start | bytes 3076
  17.2 1.5 copy-start.6
  17.3 1.4 copy-start.9
  33.4 2.4 %copy-start.7 = (f32[4,256,256]{2,1,0:T(8,128)S(1)}, f32[4,256,256]{2,1,0:T(8,128)}, u32[]{:S(2)}) copy-start(f32[4,256,256]{2,1,0:T(8,128)} %copy-done.6) | copy-start | bytes 3145732
  33.4 2.4 %copy-start.10 = (f32[256,256]{1,0:T(8,128)S(1)}, f32[256,256]{1,0:T(8,128)}, u32[]{:S(2)}) copy-start(f32[256,256]{1,0:T(8,128)} %copy-done.9) | copy-start | bytes 786436
  37.2 1.9 %copy-start.4 = (f32[256,256]{0,1:T(8,128)S(1)}, f32[256,256]{0,1:T(8,128)}, u32[]{:S(2)}) copy-start(f32[256,256]{0,1:T(8,128)} %get-tuple-element.30) | copy-start | bytes 786436
  39.9 3.7 %copy-start.2 = (f32[256,1024]{1,0:T(8,128)S(1)}, f32[256,1024]{1,0:T(8,128)}, u32[]{:S(2)}) copy-start(f32[256,1024]{1,0:T(8,128)} %copy-done.1) | copy-start | bytes 3145732
  43.6 4.4 %copy-start.5 = (f32[256,4,64]{0,2,1:T(8,128)S(1)}, f32[256,4,64]{0,2,1:T(8,128)}, u32[]{:S(2)}) copy-start(f32[256,4,64]{0,2,1:T(8,128)} %get-tuple-element.24) | copy-start | bytes 786436
  47.9 110.2 %all-reduce.6.cloned.1.call-start = ((), (), s32[]{:S(2)}) async-start(), calls=%async_computation.3 | async-start | bytes 5242880 | tf_op jit(solution)/shard_map/psum | solution.py:70
  55.3 0.7 copy-start.14
  55.3 9.1 %copy-start.3 = (f32[256,512]{1,0:T(8,128)S(1)}, f32[256,512]{1,0:T(8,128)}, u32[]{:S(2)}) copy-start(f32[256,512]{1,0:T(8,128)} %param.9) | copy-start | bytes 1572868
  55.3 9.1 %copy-start.13 = (s32[256]{0:T(256)S(1)}, s32[256]{0:T(256)}, u32[]{:S(2)}) copy-start(s32[256]{0:T(256)} %param.11) | copy-start | bytes 3076
  55.3 81.0 %copy-start.12 = (f32[1,512]{1,0:T(1,128)S(1)}, f32[1,512]{1,0:T(1,128)}, u32[]{:S(2)}) copy-start(f32[1,512]{1,0:T(1,128)} %param.14) | copy-start | bytes 6148
  128.0 7.0 %all-to-all-start = ((f32[2,1,256]{2,1,0:T(1,128)}), f32[2,1,256]{2,1,0:T(1,128)S(1)}, u32[]{:S(2)}, u32[]{:S(2)}) async-start(f32[2,1,256]{2,1,0:T(1,128)} %copy.27), calls=%async_computation.1 | async-start | bytes 4096 | tf_op jit(solution)/shard_map/all_to_all | solution.py:81
  158.2 2.9 %copy-start.8 = (f32[256,512]{1,0:T(8,128)S(1)}, f32[256,512]{1,0:T(8,128)}, u32[]{:S(2)}) copy-start(f32[256,512]{1,0:T(8,128)} %get-tuple-element.34) | copy-start | bytes 1572868
Sparse Core Ops, SparseCore 0:
  48.1 16.3 reduce-scatter.1
Sparse Core Ops, SparseCore 1:
  55.4 102.7 all-reduce.5
where the time goes:
time: 171 us; the launch traced here: 170 us
  blocking collectives  72.7 us (43%)
  waiting for transfers between devices  31.6 us (18%)
  matrix products  26.4 us (15%)
  between operations  18.8 us (11%)
  local copies, waits for them, and re-layouts  12.8 us (7%)
  other arithmetic  4.85 us (3%)
  starting transfers between devices  3.3 us (2%)
    unnamed x1, blocking collectives  61.7 us
    psum x1, waiting for transfers between devices, body(): w_uvqk_grad, w_out_grad = lax.psum((w_uvqk_part, w_out_part), 'dp')  21.2 us
    dot_general x5, matrix products, mdot(): jnp.dot(left, right, precision=highest, preferred_element_type=jnp.float32)  17.1 us
    reduce_scatter x1, waiting for transfers between devices, body(): lax.psum_scatter(head_part, 'mp', scatter_dimension=1, tiled=True)  7.24 us
    unnamed x33, local copies, waits for them, and re-layouts  6.53 us
    psum x1, blocking collectives, body(): sums = lax.psum((jnp.sum(outv, axis=1), jnp.sum(outv * outv, axis=1)), 'mp')  5.86 us
    psum x1, blocking collectives, body(): lax.psum((jnp.sum(dnorm, axis=1), jnp.sum(dnorm * normed, axis=1)), 'mp')  5.11 us
    another operation x2, local copies, waits for them, and re-layouts, body(): dact = jnp.stack([dublk, dvblk, dqblk, dkblk], axis=2)  3.65 us
  transfers between devices with their start and end apart: 3, of which 3 were waited for; matrix products, arithmetic and copies ran while one was open for 6% of the time, Pallas kernels for 0%

commit v1 on v0

v1 whole, which is shorter than its diff:
```python
import functools

import jax
import jax.numpy as jnp
from jax import lax
from jax.experimental import pallas as pl
from jax.experimental.pallas import tpu as pltpu
from jax.sharding import PartitionSpec as P

HEAD_DIM = 64
BLOCK = 4 * HEAD_DIM
MESH = pl.DeviceIdType.MESH
F32, BF16 = jnp.float32, jnp.bfloat16

NN = (((1,), (0,)), ((), ()))
NT = (((1,), (1,)), ((), ()))
TN = (((0,), (0,)), ((), ()))


def halves(value):
    high = value.astype(BF16)
    return high, (value - high.astype(F32)).astype(BF16)


def dot(left, right, dims):
    return lax.dot_general(left, right, dims, preferred_element_type=F32)


def dot3(left, right, dims):
    return dot(left[0], right[1], dims) + dot(left[1], right[0], dims) + dot(left[0], right[0], dims)


def kernel(
    n_z, n_mp, fuse,
    x_ref, g_ref, seg_ref, ids_ref, w_ref, wo_ref, table_ref, accum_ref,
    out, wopart_ref, newt_ref, newa_ref,
    buf, xt_hi, xt_lo, act, dsilu, attn, dsfac, outv, dzs, stat, stat_in,
    rc, rx, rz, sl, slc, slx, slz, slq, slm,
    ps, pr, zs, zr, ls, lr, lzs, lzr, ms, mr,
):
    count, width = x_ref.shape
    heads = w_ref.shape[1] // BLOCK
    rows = sl.shape[0]
    own = table_ref.shape[0]
    off = 1 if fuse else 0
    pieces = heads + off
    half = buf.shape[1] // 2
    quarter = half // 2
    chunk = quarter // n_z
    scale = HEAD_DIM ** (-0.5)

    dp, mp = lax.axis_index("dp"), lax.axis_index("mp")
    z, x, c = dp // 4, (dp // 2) % 2, dp % 2
    at_core = {"dp": z * 4 + x * 2 + (1 - c)}
    at_x = {"dp": z * 4 + (1 - x) * 2 + c}
    z_of = [lax.rem(z + k, n_z) for k in range(1, n_z)]
    at_z = [{"dp": zz * 4 + x * 2 + c} for zz in z_of]
    at_mp = [{"mp": lax.rem(mp + k, n_mp)} for k in range(1, n_mp)]

    barrier = pltpu.get_barrier_semaphore()
    partners = [at_core, at_x] + at_z + at_mp
    for partner in partners:
        pl.semaphore_signal(barrier, inc=1, device_id=partner, device_id_type=MESH)

    def remote(src, dst, send, recv, where):
        return pltpu.make_async_remote_copy(
            src_ref=src, dst_ref=dst, send_sem=send, recv_sem=recv, device_id=where, device_id_type=MESH
        )

    def span(start, size):
        return pl.ds(pl.multiple_of(start, 8), size)

    mine = span(c * half, half)
    theirs = span((1 - c) * half, half)
    my_q = span(c * half + x * quarter, quarter)
    their_q = span(c * half + (1 - x) * quarter, quarter)
    my_chunk = span(c * half + x * quarter + z * chunk, chunk)

    def core_rs(p):
        return remote(buf.at[p, theirs], rc.at[p], ps.at[0, p], pr.at[0, p], at_core)

    def x_rs(p):
        return remote(buf.at[p, their_q], rx.at[p], ps.at[1, p], pr.at[1, p], at_x)

    def z_rs(p, k):
        part = span(c * half + x * quarter + z_of[k] * chunk, chunk)
        return remote(buf.at[p, part], rz.at[p, k], zs.at[0, p, k], zr.at[0, p, k], at_z[k])

    def z_ag(p, k):
        return remote(out.at[p, my_chunk], out.at[p, my_chunk], zs.at[1, p, k], zr.at[1, p, k], at_z[k])

    def x_ag(p):
        return remote(out.at[p, my_q], out.at[p, my_q], ps.at[2, p], pr.at[2, p], at_x)

    def core_ag(p):
        return remote(out.at[p, mine], out.at[p, mine], ps.at[3, p], pr.at[3, p], at_core)

    def stage(s, p):
        if s == 0:
            core_rs(p).start()
        elif s == 1:
            core_rs(p).wait()
            buf[p, their_q] += rc[p, span((1 - x) * quarter, quarter)]
            x_rs(p).start()
            buf[p, my_q] += rc[p, span(x * quarter, quarter)]
        elif s == 2:
            x_rs(p).wait()
            buf[p, my_q] += rx[p]
            for k in range(n_z - 1):
                z_rs(p, k).start()
        elif s == 3:
            total = buf[p, my_chunk]
            for k in range(n_z - 1):
                z_rs(p, k).wait()
                total = total + rz[p, k]
            out[p, my_chunk] = total
            for k in range(n_z - 1):
                z_ag(p, k).start()
        elif s == 4:
            for k in range(n_z - 1):
                z_ag(p, k).wait()
            x_ag(p).start()
        elif s == 5:
            x_ag(p).wait()
            core_ag(p).start()
        else:
            core_ag(p).wait()

    seg = jnp.broadcast_to(seg_ref[...].astype(F32), (count, count))
    spot = lax.broadcasted_iota(jnp.int32, (count, count), 0)
    other = lax.broadcasted_iota(jnp.int32, (count, count), 1)
    mask = jnp.where((seg == seg.T) & (spot >= other), 1.0, 0.0)
    xs = halves(x_ref[...])
    gs = halves(g_ref[...])

    def forward(h, sums):
        ws = halves(w_ref[:, pl.ds(pl.multiple_of(h * BLOCK, BLOCK), BLOCK)])
        pre = dot3(xs, ws, NN)
        sig = jax.nn.sigmoid(pre)
        val = pre * sig
        act[h] = val
        dsilu[h] = sig * (1.0 + pre * (1.0 - sig))
        u, v = val[:, 0:64], val[:, 64:128]
        q, k = val[:, 128:192], val[:, 192:256]
        score = dot3(halves(q), halves(k), NT) * scale
        ssig = jax.nn.sigmoid(score)
        a = score * ssig * mask
        attn[h] = a
        dsfac[h] = mask * (ssig * (1.0 + score * (1.0 - ssig))) * scale
        o = dot3(halves(a), halves(v), NN)
        outv[h] = o
        wos = halves(wo_ref[pl.ds(pl.multiple_of(h * HEAD_DIM, HEAD_DIM), HEAD_DIM), :])
        dz = dot3(gs, wos, NT)
        dzs[h] = dz
        dn = dz * u
        return (sums[0] + o, sums[1] + o * o, sums[2] + dn, sums[3] + dn * o)

    zero = jnp.zeros((count, HEAD_DIM), F32)
    sums = lax.fori_loop(0, heads, forward, (zero, zero, zero, zero))
    lane = lax.broadcasted_iota(jnp.int32, (count, 128), 1)
    packed = jnp.zeros((count, 128), F32)
    for i in range(4):
        packed = jnp.where(lane == i, jnp.sum(sums[i], axis=1, keepdims=True), packed)
    stat[...] = packed.T[0:8]
    pl.semaphore_wait(barrier, len(partners))

    def stat_to(k):
        return remote(stat, stat_in.at[k], ms.at[0, k], mr.at[0, k], at_mp[k])

    for k in range(n_mp - 1):
        stat_to(k).start()
    x_t = x_ref[...].T
    xt_hi[...], xt_lo[...] = halves(x_t)
    place = lax.broadcasted_iota(jnp.int32, (rows, count), 0)
    inner = n_z * n_mp * own
    pc, px = place // (2 * inner), (place // inner) % 2
    pz, pm = (place // (n_mp * own)) % n_z, place % (n_mp * own)
    wanted = ((pz * 2 + px) * 2 + pc) * (n_mp * own) + pm
    hits = jnp.where(wanted == ids_ref[...], 1.0, 0.0).astype(BF16)
    sl[...] = (dot(hits, gs[0], NN) + dot(hits, gs[1], NN)) * (1.0 / n_mp)

    total = stat[...]
    for k in range(n_mp - 1):
        stat_to(k).wait()
        total = total + stat_in[k]
    cols = jnp.concatenate([total, jnp.zeros((120, count), F32)], axis=0).T
    mean = cols[:, 0:1] / width
    var = cols[:, 1:2] / width - mean * mean
    rstd = lax.rsqrt(var + 1e-05)
    m1 = cols[:, 2:3] / width
    m2 = rstd * (cols[:, 3:4] - mean * cols[:, 2:3]) / width

    z_all = jnp.concatenate(
        [(outv[h] - mean) * rstd * act[h][:, 0:64] for h in range(heads)], axis=1
    )
    wo_grad = dot3(halves(z_all), gs, TN)
    if fuse:
        buf[0, 0:half] = wo_grad[:, 0:BLOCK]
        buf[0, half : 2 * half] = wo_grad[:, BLOCK : 2 * BLOCK]
        stage(0, 0)
        wopart_ref[...] = jnp.zeros(wopart_ref.shape, F32)
    else:
        wopart_ref[...] = wo_grad

    def backward(h, carry):
        val = act[h]
        u, v = val[:, 0:64], val[:, 64:128]
        q, k = val[:, 128:192], val[:, 192:256]
        nrm = (outv[h] - mean) * rstd
        dz = dzs[h]
        dn = dz * u
        du = dz * nrm
        do = halves(rstd * (dn - m1 - nrm * m2))
        da = dot3(do, halves(v), NT)
        dv = dot3(halves(attn[h]), do, TN)
        ds = halves(da * dsfac[h])
        dq = dot3(ds, halves(k), NN)
        dk = dot3(ds, halves(q), TN)
        dpre = halves(jnp.concatenate([du, dv, dq, dk], axis=1) * dsilu[h])
        buf[h + off] = dot3((xt_hi[...], xt_lo[...]), dpre, NN)
        stage(0, h + off)
        rowsum = dot(hits, dpre[0], NN) + dot(hits, dpre[1], NN)
        ws = halves(w_ref[:, pl.ds(pl.multiple_of(h * BLOCK, BLOCK), BLOCK)])
        sl[...] += dot3(halves(rowsum), ws, NT)
        for s in range(1, min(6, heads - 1 + off) + 1):
            if off == 1 and s == 1:
                stage(s, h)
            else:
                pl.when(h + off - s >= 0)(functools.partial(stage, s, h + off - s))
        return carry

    lax.fori_loop(0, heads, backward, 0)

    s_half, s_q = rows // 2, rows // 4
    s_mine = span(c * s_half + x * s_q, s_q)

    def sl_core():
        return remote(sl.at[span((1 - c) * s_half, s_half)], slc, ls.at[0], lr.at[0], at_core)

    def sl_x():
        return remote(sl.at[span(c * s_half + (1 - x) * s_q, s_q)], slx, ls.at[1], lr.at[1], at_x)

    def sl_z(k):
        return remote(sl.at[s_mine], slz.at[k], lzs.at[k], lzr.at[k], at_z[k])

    def sl_mp(k):
        return remote(slq, slm.at[k], ms.at[1, k], mr.at[1, k], at_mp[k])

    def slab(t):
        if t == 0:
            sl_core().start()
        elif t == 1:
            sl_core().wait()
            sl[span(c * s_half, s_half)] += slc[...]
            sl_x().start()
        elif t == 2:
            sl_x().wait()
            sl[s_mine] += slx[...]
            for k in range(n_z - 1):
                sl_z(k).start()
        elif t == 3:
            part = sl[s_mine]
            for k in range(n_z - 1):
                sl_z(k).wait()
                part = part + slz[k]
            slq[...] = part
            for k in range(n_mp - 1):
                sl_mp(k).start()
        elif t == 4:
            part = slq[pl.ds((z * n_mp + mp) * own, own), :]
            for k in range(n_mp - 1):
                sl_mp(k).wait()
                part = part + slm[k, pl.ds((z * n_mp + mp) * own, own), :]
            newa = accum_ref[...] + jnp.sum(part * part, axis=1, keepdims=True) / width
            newa_ref[...] = newa
            newt_ref[...] = table_ref[...] - 0.5 * part * lax.rsqrt(newa)

    slab(0)
    for t in range(1, 7):
        tick = heads - 1 + off + t
        for s in range(0, 7):
            if 0 <= tick - s < pieces:
                stage(s, tick - s)
        slab(t)


def body(layer_input, grad_out, segment, item_ids, w_uvqk, w_out, table, accum):
    count, width = layer_input.shape
    cols = w_uvqk.shape[1]
    heads = cols // BLOCK
    feats = heads * HEAD_DIM
    n_dp, n_mp = lax.axis_size("dp"), lax.axis_size("mp")
    own = table.shape[0]
    rows = own * n_dp * n_mp
    n_z = n_dp // 4
    fuse = feats * width == width * BLOCK
    pieces = heads + (1 if fuse else 0)
    half, quarter = width // 2, width // 4
    chunk = quarter // n_z
    wo_shape = (8, 128) if fuse else (feats, width)
    vmem = pl.BlockSpec(memory_space=pltpu.VMEM)
    dma = pltpu.SemaphoreType.DMA
    out, wo_part, new_table, new_accum = pl.pallas_call(
        functools.partial(kernel, n_z, n_mp, fuse),
        out_shape=(
            jax.ShapeDtypeStruct((pieces, width, BLOCK), F32),
            jax.ShapeDtypeStruct(wo_shape, F32),
            jax.ShapeDtypeStruct((own, width), F32),
            jax.ShapeDtypeStruct((own, 1), F32),
        ),
        in_specs=[vmem] * 8,
        out_specs=(vmem,) * 4,
        scratch_shapes=[
            pltpu.VMEM((pieces, width, BLOCK), F32),
            pltpu.VMEM((width, count), BF16),
            pltpu.VMEM((width, count), BF16),
            pltpu.VMEM((heads, count, BLOCK), F32),
            pltpu.VMEM((heads, count, BLOCK), F32),
            pltpu.VMEM((heads, count, count), F32),
            pltpu.VMEM((heads, count, count), F32),
            pltpu.VMEM((heads, count, HEAD_DIM), F32),
            pltpu.VMEM((heads, count, HEAD_DIM), F32),
            pltpu.VMEM((8, count), F32),
            pltpu.VMEM((n_mp - 1, 8, count), F32),
            pltpu.VMEM((pieces, half, BLOCK), F32),
            pltpu.VMEM((pieces, quarter, BLOCK), F32),
            pltpu.VMEM((pieces, n_z - 1, chunk, BLOCK), F32),
            pltpu.VMEM((rows, width), F32),
            pltpu.VMEM((rows // 2, width), F32),
            pltpu.VMEM((rows // 4, width), F32),
            pltpu.VMEM((n_z - 1, rows // 4, width), F32),
            pltpu.VMEM((rows // 4, width), F32),
            pltpu.VMEM((n_mp - 1, rows // 4, width), F32),
            dma((4, pieces)),
            dma((4, pieces)),
            dma((2, pieces, n_z - 1)),
            dma((2, pieces, n_z - 1)),
            dma((2,)),
            dma((2,)),
            dma((n_z - 1,)),
            dma((n_z - 1,)),
            dma((2, n_mp - 1)),
            dma((2, n_mp - 1)),
        ],
        compiler_params=pltpu.CompilerParams(
            collective_id=0, has_side_effects=True, vmem_limit_bytes=40 * 1024 * 1024
        ),
    )(
        layer_input,
        grad_out,
        segment,
        item_ids.reshape(1, count),
        w_uvqk,
        w_out,
        table,
        accum.reshape(own, 1),
    )
    w_uvqk_grad = jnp.concatenate([out[p] for p in range(pieces - heads, pieces)], axis=1)
    if fuse:
        w_out_grad = jnp.concatenate([out[0, :feats], out[0, feats:]], axis=1)
    else:
        w_out_grad = lax.psum(wo_part, "dp")
    return w_uvqk_grad, w_out_grad, new_table, new_accum.reshape(own)


def solution(mesh):
    placed = (
        P("dp", None),
        P("dp", None),
        P("dp", None),
        P("dp"),
        P(None, "mp"),
        P("mp", None),
        P(("dp", "mp"), None),
        P(("dp", "mp")),
    )
    return jax.shard_map(
        body,
        mesh=mesh,
        in_specs=placed,
        out_specs=(P(None, "mp"), P("mp", None), P(("dp", "mp"), None), P(("dp", "mp"))),
        check_vma=False,
    )
```

time: 171 us -> 70 us (0.41)
  blocking collectives: 72.7 us -> 0 us
  Pallas kernels: 0 us -> 56.6 us
  waiting for transfers between devices: 31.6 us -> 0 us
  matrix products: 26.4 us -> 0 us
  between operations: 18.8 us -> 3.08 us
  local copies, waits for them, and re-layouts: 12.8 us -> 7.5 us
  starting transfers between devices: 3.3 us -> 0 us
  other arithmetic: 4.85 us -> 2.43 us
    unnamed x1 -> x0, blocking collectives: 61.7 us -> none
    pallas_call x0 -> x1, Pallas kernels: none -> 56.6 us  [body(): pl.pallas_call(functools.partial(kernel, n_z, n_mp, fuse), out_shape=(jax...]
    dot_general x12 -> x0, matrix products: 26.4 us -> none  [the longest x5 17.1 us: mdot(): jnp.dot(left, right, precision=highest, preferred_element_type=jnp.float32)]
    psum x1 -> x0, waiting for transfers between devices: 21.2 us -> none  [body(): w_uvqk_grad, w_out_grad = lax.psum((w_uvqk_part, w_out_part), 'dp')]
    psum x2 -> x0, blocking collectives: 11 us -> none  [the longest x1 5.86 us: body(): sums = lax.psum((jnp.sum(outv, axis=1), jnp.sum(outv * outv, axis=1)), 'mp')]
    reduce_scatter x1 -> x0, waiting for transfers between devices: 7.24 us -> none  [body(): lax.psum_scatter(head_part, 'mp', scatter_dimension=1, tiled=True)]
    another operation x2 -> x0, local copies, waits for them, and re-layouts: 3.65 us -> none  [body(): dact = jnp.stack([dublk, dvblk, dqblk, dkblk], axis=2)]
    mul x4 -> x0, other arithmetic: 3.41 us -> none  [the longest x1 1.53 us: body(): act = jax.nn.silu(pre)]
  transfers between devices with their start and end apart: 3 -> 0, of which waited for: 3 -> 0; matrix products, arithmetic and copies ran while one was open for 6% -> 0% of each run, Pallas kernels for 0% -> 0%
where the time goes in v1:
time: 70 us; the launch traced here: 69.6 us
  Pallas kernels  56.6 us (81%)
  local copies, waits for them, and re-layouts  7.5 us (11%)
  between operations  3.08 us (4%)
  other arithmetic  2.43 us (3%)
    pallas_call x1, Pallas kernels, body(): pl.pallas_call(functools.partial(kernel, n_z, n_mp, fuse), out_shape=(jax...  56.6 us
    unnamed x15, local copies, waits for them, and re-layouts  7.32 us
    concatenate x1, other arithmetic, body(): jnp.concatenate([out[p] for p in range(pieces - heads, pieces)], axis=1)  1.58 us

profile of v1, /device:TPU:0, one launch (start us, length us, event | category | flops | bytes accessed | tf_op | source)
XLA Modules:
  0.0 69.6 jit_solution(16861359611712536396)
XLA Ops:
  1.3 0.0 copy-start
  1.3 1.6 %copy-done = f32[512,1024]{1,0:T(8,128)S(1)} copy-done((f32[512,1024]{1,0:T(8,128)S(1)}, f32[512,1024]{1,0:T(8,128)}, u32[]{:S(2)}) %copy-start) | copy-done | bytes 2097176
  2.9 0.0 copy-start.1
  2.9 1.0 %copy-done.1 = f32[256,512]{1,0:T(8,128)S(1)} copy-done((f32[256,512]{1,0:T(8,128)S(1)}, f32[256,512]{1,0:T(8,128)}, u32[]{:S(2)}) %copy-start.1) | copy-done | bytes 524312
  3.9 0.0 copy-start.2
  3.9 1.0 %copy-done.2 = f32[256,512]{1,0:T(8,128)S(1)} copy-done((f32[256,512]{1,0:T(8,128)S(1)}, f32[256,512]{1,0:T(8,128)}, u32[]{:S(2)}) %copy-start.2) | copy-done | bytes 524312
  5.0 0.0 copy-start.3
  5.0 1.0 %copy-done.3 = f32[256,512]{1,0:T(8,128)S(1)} copy-done((f32[256,512]{1,0:T(8,128)S(1)}, f32[256,512]{1,0:T(8,128)}, u32[]{:S(2)}) %copy-start.3) | copy-done | bytes 524312
  6.0 0.0 copy-start.4
  6.0 0.7 copy-done.4
  6.7 0.0 copy-start.5
  6.7 0.7 copy-done.5
  7.4 0.0 copy-start.6
  7.4 0.7 copy-done.6
  8.0 56.6 %shard_map.111 = (f32[5,512,256]{2,1,0:T(8,128)S(1)}, f32[8,128]{1,0:T(8,128)}, f32[1,512]{1,0:T(1,128)S(1)}, f32[1,1]{1,0:T(1,128)}) custom-call(f32[256,512]{1,0:T(8,128)S(1)} %copy-done.1, f32[256,512]{1,0:T(8,128)S(1)} %copy-done.2, s32[1,256]{1,0:T(1,128)S(1)} %copy-done.5, s32[1,256]{1,0:T(1,128)S(1)} %bitcast.16, f32[512,1024]{1,0:T(8,128)S(1)} %copy-done, ...), custom_call_target="tpu_custom_call" | custom-call | tf_op jit(solution)/shard_map/pallas_call | solution.py:303
  64.7 0.1 slice_bitcast_fusion.3
  64.8 1.6 %pad_maximum_fusion = f32[512,1024]{1,0:T(8,128)} fusion(f32[512,256]{1,0:T(8,128)S(1)} %get-tuple-element.13, f32[512,256]{1,0:T(8,128)S(1)} %get-tuple-element.14, f32[512,256]{1,0:T(8,128)S(1)} %get-tuple-element.15, f32[512,256]{1,0:T(8,128)S(1)} %get-tuple-element.12), kind=kLoop, calls=%fused_computation | loop fusion | flops 1572864 | bytes 4194304 | tf_op jit(solution)/shard_map/concatenate | solution.py:358
  66.4 0.9 %pad_maximum_fusion.1 = f32[256,512]{1,0:T(8,128)} fusion(f32[256,256]{1,0:T(8,128)S(1)} %get-tuple-element.11, f32[256,256]{1,0:T(8,128)S(1)} %get-tuple-element.10), kind=kLoop, calls=%fused_computation.1 | loop fusion | flops 131072 | bytes 1048576 | tf_op jit(solution)/shard_map/concatenate | solution.py:360
  67.3 0.6 copy.15
  (1 shorter events, 0.0 us)
Async XLA Ops:
  1.3 1.6 %copy-start = (f32[512,1024]{1,0:T(8,128)S(1)}, f32[512,1024]{1,0:T(8,128)}, u32[]{:S(2)}) copy-start(f32[512,1024]{1,0:T(8,128)} %w_ref.1) | copy-start | bytes 6291460
  2.9 1.0 %copy-start.1 = (f32[256,512]{1,0:T(8,128)S(1)}, f32[256,512]{1,0:T(8,128)}, u32[]{:S(2)}) copy-start(f32[256,512]{1,0:T(8,128)} %x_ref.1) | copy-start | bytes 1572868
  3.9 1.0 %copy-start.2 = (f32[256,512]{1,0:T(8,128)S(1)}, f32[256,512]{1,0:T(8,128)}, u32[]{:S(2)}) copy-start(f32[256,512]{1,0:T(8,128)} %g_ref.1) | copy-start | bytes 1572868
  5.0 1.0 %copy-start.3 = (f32[256,512]{1,0:T(8,128)S(1)}, f32[256,512]{1,0:T(8,128)}, u32[]{:S(2)}) copy-start(f32[256,512]{1,0:T(8,128)} %wo_ref.1) | copy-start | bytes 1572868
  6.0 0.7 copy-start.4
  6.7 0.7 copy-start.5
  7.4 0.7 copy-start.6

commit v2 on v1

--- a/solution.py
+++ b/solution.py
@@ -31,30 +31,37 @@
 
 
 def kernel(
-    n_z, n_mp, fuse,
-    x_ref, g_ref, seg_ref, ids_ref, w_ref, wo_ref, table_ref, accum_ref,
+    n_bits, n_z, n_mp, fuse, split,
+    x_hbm, g_hbm, seg_hbm, ids_hbm, w_hbm, wo_hbm, table_hbm, accum_ref,
     out, wopart_ref, newt_ref, newa_ref,
+    x_ref, g_ref, seg_ref, ids_ref, w_ref, wo_ref, table_ref, in_sem,
     buf, xt_hi, xt_lo, act, dsilu, attn, dsfac, outv, dzs, stat, stat_in,
-    rc, rx, rz, sl, slc, slx, slz, slq, slm,
-    ps, pr, zs, zr, ls, lr, lzs, lzr, ms, mr,
+    sl, slc, slx, slz, slq, slm,
+    ps, pr, ls, lr, lzs, lzr, ms, mr,
+    *rcv,
 ):
+    loads = []
+    for i, (src, dst) in enumerate((
+        (seg_hbm, seg_ref), (x_hbm, x_ref), (w_hbm, w_ref), (g_hbm, g_ref),
+        (wo_hbm, wo_ref), (ids_hbm, ids_ref), (table_hbm, table_ref),
+    )):
+        loads.append(pltpu.make_async_copy(src, dst, in_sem.at[i]))
+        loads[-1].start()
+
     count, width = x_ref.shape
     heads = w_ref.shape[1] // BLOCK
     rows = sl.shape[0]
     own = table_ref.shape[0]
     off = 1 if fuse else 0
-    pieces = heads + off
-    half = buf.shape[1] // 2
-    quarter = half // 2
-    chunk = quarter // n_z
+    pieces, size = buf.shape[0], buf.shape[1]
     scale = HEAD_DIM ** (-0.5)
 
     dp, mp = lax.axis_index("dp"), lax.axis_index("mp")
     z, x, c = dp // 4, (dp // 2) % 2, dp % 2
-    at_core = {"dp": z * 4 + x * 2 + (1 - c)}
-    at_x = {"dp": z * 4 + (1 - x) * 2 + c}
-    z_of = [lax.rem(z + k, n_z) for k in range(1, n_z)]
-    at_z = [{"dp": zz * 4 + x * 2 + c} for zz in z_of]
+    bit = [(dp // 2**i) % 2 for i in range(n_bits)]
+    flip = [dp + (1 - 2 * bit[i]) * 2**i for i in range(n_bits)]
+    at_core, at_x = {"dp": flip[0]}, {"dp": flip[1]}
+    at_z = [{"dp": lax.rem(z + k, n_z) * 4 + x * 2 + c} for k in range(1, n_z)]
     at_mp = [{"mp": lax.rem(mp + k, n_mp)} for k in range(1, n_mp)]
 
     barrier = pltpu.get_barrier_semaphore()
@@ -67,71 +74,64 @@
             src_ref=src, dst_ref=dst, send_sem=send, recv_sem=recv, device_id=where, device_id_type=MESH
         )
 
-    def span(start, size):
-        return pl.ds(pl.multiple_of(start, 8), size)
-
-    mine = span(c * half, half)
-    theirs = span((1 - c) * half, half)
-    my_q = span(c * half + x * quarter, quarter)
-    their_q = span(c * half + (1 - x) * quarter, quarter)
-    my_chunk = span(c * half + x * quarter + z * chunk, chunk)
-
-    def core_rs(p):
-        return remote(buf.at[p, theirs], rc.at[p], ps.at[0, p], pr.at[0, p], at_core)
-
-    def x_rs(p):
-        return remote(buf.at[p, their_q], rx.at[p], ps.at[1, p], pr.at[1, p], at_x)
-
-    def z_rs(p, k):
-        part = span(c * half + x * quarter + z_of[k] * chunk, chunk)
-        return remote(buf.at[p, part], rz.at[p, k], zs.at[0, p, k], zr.at[0, p, k], at_z[k])
-
-    def z_ag(p, k):
-        return remote(out.at[p, my_chunk], out.at[p, my_chunk], zs.at[1, p, k], zr.at[1, p, k], at_z[k])
-
-    def x_ag(p):
-        return remote(out.at[p, my_q], out.at[p, my_q], ps.at[2, p], pr.at[2, p], at_x)
-
-    def core_ag(p):
-        return remote(out.at[p, mine], out.at[p, mine], ps.at[3, p], pr.at[3, p], at_core)
+    def span(start, length):
+        return pl.ds(pl.multiple_of(start, 8), length)
+
+    def step(p, i):
+        swap = (p % 4) // 3
+        bits = [bit[0], bit[1] + swap * (bit[2] - bit[1]), bit[2] + swap * (bit[1] - bit[2])] + bit[3:]
+        to = [flip[0], flip[1] + swap * (flip[2] - flip[1]), flip[2] + swap * (flip[1] - flip[2])] + flip[3:]
+        start = 0
+        for j in range(i):
+            start = start + bits[j] * (size >> (j + 1))
+        return bits[i], {"dp": to[i]}, start
+
+    def reduce_copy(p, i):
+        b, where, start = step(p, i)
+        length = size >> (i + 1)
+        return remote(
+            buf.at[p, span(start + (1 - b) * length, length)], rcv[i].at[p], ps.at[i, p], pr.at[i, p], where
+        )
+
+    def gather_copy(p, i):
+        b, where, start = step(p, i)
+        length = size >> (i + 1)
+        at = span(start + b * length, length)
+        return remote(out.at[p, at], out.at[p, at], ps.at[n_bits + i, p], pr.at[n_bits + i, p], where)
 
     def stage(s, p):
         if s == 0:
-            core_rs(p).start()
-        elif s == 1:
-            core_rs(p).wait()
-            buf[p, their_q] += rc[p, span((1 - x) * quarter, quarter)]
-            x_rs(p).start()
-            buf[p, my_q] += rc[p, span(x * quarter, quarter)]
-        elif s == 2:
-            x_rs(p).wait()
-            buf[p, my_q] += rx[p]
-            for k in range(n_z - 1):
-                z_rs(p, k).start()
-        elif s == 3:
-            total = buf[p, my_chunk]
-            for k in range(n_z - 1):
-                z_rs(p, k).wait()
-                total = total + rz[p, k]
-            out[p, my_chunk] = total
-            for k in range(n_z - 1):
-                z_ag(p, k).start()
-        elif s == 4:
-            for k in range(n_z - 1):
-                z_ag(p, k).wait()
-            x_ag(p).start()
-        elif s == 5:
-            x_ag(p).wait()
-            core_ag(p).start()
+            reduce_copy(p, 0).start()
+        elif s < n_bits:
+            reduce_copy(p, s - 1).wait()
+            b, _, start = step(p, s)
+            length = size >> (s + 1)
+            buf[p, span(start + (1 - b) * length, length)] += rcv[s - 1][p, span((1 - b) * length, length)]
+            reduce_copy(p, s).start()
+            buf[p, span(start + b * length, length)] += rcv[s - 1][p, span(b * length, length)]
+        elif s == n_bits:
+            reduce_copy(p, s - 1).wait()
+            b, _, start = step(p, s - 1)
+            at = span(start + b * (size >> s), size >> s)
+            out[p, at] = buf[p, at] + rcv[s - 1][p]
+            gather_copy(p, s - 1).start()
         else:
-            core_ag(p).wait()
-
+            i = 2 * n_bits - s
+            gather_copy(p, i).wait()
+            if i > 0:
+                gather_copy(p, i - 1).start()
+
+    loads[0].wait()
     seg = jnp.broadcast_to(seg_ref[...].astype(F32), (count, count))
     spot = lax.broadcasted_iota(jnp.int32, (count, count), 0)
     other = lax.broadcasted_iota(jnp.int32, (count, count), 1)
     mask = jnp.where((seg == seg.T) & (spot >= other), 1.0, 0.0)
+    loads[1].wait()
     xs = halves(x_ref[...])
+    loads[3].wait()
     gs = halves(g_ref[...])
+    loads[2].wait()
+    loads[4].wait()
 
     def forward(h, sums):
         ws = halves(w_ref[:, pl.ds(pl.multiple_of(h * BLOCK, BLOCK), BLOCK)])
@@ -169,6 +169,8 @@
 
     for k in range(n_mp - 1):
         stat_to(k).start()
+    loads[5].wait()
+    loads[6].wait()
     x_t = x_ref[...].T
     xt_hi[...], xt_lo[...] = halves(x_t)
     place = lax.broadcasted_iota(jnp.int32, (rows, count), 0)
@@ -195,12 +197,25 @@
     )
     wo_grad = dot3(halves(z_all), gs, TN)
     if fuse:
-        buf[0, 0:half] = wo_grad[:, 0:BLOCK]
-        buf[0, half : 2 * half] = wo_grad[:, BLOCK : 2 * BLOCK]
-        stage(0, 0)
+        for i in range(2):
+            for j in range(split // 2):
+                buf[i * (split // 2) + j] = wo_grad[j * size : (j + 1) * size, i * BLOCK : (i + 1) * BLOCK]
+        for p in range(split):
+            for s in range(p + 1):
+                stage(s, p - s)
         wopart_ref[...] = jnp.zeros(wopart_ref.shape, F32)
     else:
         wopart_ref[...] = wo_grad
+
+    last = split * (heads + off) - 1
+
+    def tick(piece, low):
+        stage(0, piece)
+        for s in range(1, min(2 * n_bits, last) + 1):
+            if s <= low:
+                stage(s, piece - s)
+            else:
+                pl.when(piece >= s)(functools.partial(stage, s, piece - s))
 
     def backward(h, carry):
         val = act[h]
@@ -217,16 +232,14 @@
         dq = dot3(ds, halves(k), NN)
         dk = dot3(ds, halves(q), TN)
         dpre = halves(jnp.concatenate([du, dv, dq, dk], axis=1) * dsilu[h])
-        buf[h + off] = dot3((xt_hi[...], xt_lo[...]), dpre, NN)
-        stage(0, h + off)
-        rowsum = dot(hits, dpre[0], NN) + dot(hits, dpre[1], NN)
-        ws = halves(w_ref[:, pl.ds(pl.multiple_of(h * BLOCK, BLOCK), BLOCK)])
-        sl[...] += dot3(halves(rowsum), ws, NT)
-        for s in range(1, min(6, heads - 1 + off) + 1):
-            if off == 1 and s == 1:
-                stage(s, h)
-            else:
-                pl.when(h + off - s >= 0)(functools.partial(stage, s, h + off - s))
+        for j in range(split):
+            part = slice(j * size, (j + 1) * size)
+            buf[(h + off) * split + j] = dot3((xt_hi[part], xt_lo[part]), dpre, NN)
+            if j == split - 1:
+                rowsum = dot(hits, dpre[0], NN) + dot(hits, dpre[1], NN)
+                ws = halves(w_ref[:, pl.ds(pl.multiple_of(h * BLOCK, BLOCK), BLOCK)])
+                sl[...] += dot3(halves(rowsum), ws, NT)
+            tick((h + off) * split + j, off * split + j)
         return carry
 
     lax.fori_loop(0, heads, backward, 0)
@@ -276,12 +289,12 @@
             newt_ref[...] = table_ref[...] - 0.5 * part * lax.rsqrt(newa)
 
     slab(0)
-    for t in range(1, 7):
-        tick = heads - 1 + off + t
-        for s in range(0, 7):
-            if 0 <= tick - s < pieces:
-                stage(s, tick - s)
-        slab(t)
+    for t in range(1, 2 * n_bits + 1):
+        for s in range(0, 2 * n_bits + 1):
+            if 0 <= last + t - s <= last:
+                stage(s, last + t - s)
+        if t <= 4:
+            slab(t)
 
 
 def body(layer_input, grad_out, segment, item_ids, w_uvqk, w_out, table, accum):
@@ -293,25 +306,34 @@
     own = table.shape[0]
     rows = own * n_dp * n_mp
     n_z = n_dp // 4
-    fuse = feats * width == width * BLOCK
-    pieces = heads + (1 if fuse else 0)
-    half, quarter = width // 2, width // 4
-    chunk = quarter // n_z
+    fuse = feats == BLOCK and width // 2 // n_dp >= 8
+    split = 2 if fuse else 1
+    pieces = split * (heads + (1 if fuse else 0))
+    size = width // split
+    n_bits = n_dp.bit_length() - 1
     wo_shape = (8, 128) if fuse else (feats, width)
     vmem = pl.BlockSpec(memory_space=pltpu.VMEM)
     dma = pltpu.SemaphoreType.DMA
     out, wo_part, new_table, new_accum = pl.pallas_call(
-        functools.partial(kernel, n_z, n_mp, fuse),
+        functools.partial(kernel, n_bits, n_z, n_mp, fuse, split),
         out_shape=(
-            jax.ShapeDtypeStruct((pieces, width, BLOCK), F32),
+            jax.ShapeDtypeStruct((pieces, size, BLOCK), F32),
             jax.ShapeDtypeStruct(wo_shape, F32),
             jax.ShapeDtypeStruct((own, width), F32),
             jax.ShapeDtypeStruct((own, 1), F32),
         ),
-        in_specs=[vmem] * 8,
+        in_specs=[pl.BlockSpec(memory_space=pl.ANY)] * 7 + [vmem],
         out_specs=(vmem,) * 4,
         scratch_shapes=[
-            pltpu.VMEM((pieces, width, BLOCK), F32),
+            pltpu.VMEM((count, width), F32),
+            pltpu.VMEM((count, width), F32),
+            pltpu.VMEM((1, count), jnp.int32),
+            pltpu.VMEM((1, count), jnp.int32),
+            pltpu.VMEM((width, cols), F32),
+            pltpu.VMEM((feats, width), F32),
+            pltpu.VMEM((own, width), F32),
+            dma((7,)),
+            pltpu.VMEM((pieces, size, BLOCK), F32),
             pltpu.VMEM((width, count), BF16),
             pltpu.VMEM((width, count), BF16),
             pltpu.VMEM((heads, count, BLOCK), F32),
@@ -322,28 +344,23 @@
             pltpu.VMEM((heads, count, HEAD_DIM), F32),
             pltpu.VMEM((8, count), F32),
             pltpu.VMEM((n_mp - 1, 8, count), F32),
-            pltpu.VMEM((pieces, half, BLOCK), F32),
-            pltpu.VMEM((pieces, quarter, BLOCK), F32),
-            pltpu.VMEM((pieces, n_z - 1, chunk, BLOCK), F32),
             pltpu.VMEM((rows, width), F32),
             pltpu.VMEM((rows // 2, width), F32),
             pltpu.VMEM((rows // 4, width), F32),
             pltpu.VMEM((n_z - 1, rows // 4, width), F32),
             pltpu.VMEM((rows // 4, width), F32),
             pltpu.VMEM((n_mp - 1, rows // 4, width), F32),
-            dma((4, pieces)),
-            dma((4, pieces)),
-            dma((2, pieces, n_z - 1)),
-            dma((2, pieces, n_z - 1)),
+            dma((2 * n_bits, pieces)),
+            dma((2 * n_bits, pieces)),
             dma((2,)),
             dma((2,)),
             dma((n_z - 1,)),
             dma((n_z - 1,)),
             dma((2, n_mp - 1)),
             dma((2, n_mp - 1)),
-        ],
+        ] + [pltpu.VMEM((pieces, size >> (i + 1), BLOCK), F32) for i in range(n_bits)],
         compiler_params=pltpu.CompilerParams(
-            collective_id=0, has_side_effects=True, vmem_limit_bytes=40 * 1024 * 1024
+            collective_id=0, has_side_effects=True, vmem_limit_bytes=56 * 1024 * 1024
         ),
     )(
         layer_input,
@@ -355,7 +372,8 @@
         table,
         accum.reshape(own, 1),
     )
-    w_uvqk_grad = jnp.concatenate([out[p] for p in range(pieces - heads, pieces)], axis=1)
+    out = out.reshape(pieces // split, width, BLOCK)
+    w_uvqk_grad = jnp.concatenate([out[p] for p in range(pieces // split - heads, pieces // split)], axis=1)
     if fuse:
         w_out_grad = jnp.concatenate([out[0, :feats], out[0, feats:]], axis=1)
     else:

time: 70 us -> 75.9 us (1.084)
  Pallas kernels: 56.6 us -> 66.9 us
  local copies, waits for them, and re-layouts: 7.5 us -> 3.3 us
    pallas_call x1, Pallas kernels: 56.6 us -> 66.9 us  [body(): pl.pallas_call(functools.partial(kernel, n_bits, n_z, n_mp, fuse, split),...]
    unnamed x15 -> x3, local copies, waits for them, and re-layouts: 7.32 us -> 0.58 us
    slice x0 -> x1, local copies, waits for them, and re-layouts: none -> 1.65 us  [body(): out[p]]
    squeeze x1, local copies, waits for them, and re-layouts: 0.04 us -> 1.07 us  [body(): w_out_grad = jnp.concatenate([out[0, :feats], out[0, feats:]], axis=1)]
where the time goes in v2:
time: 75.9 us; the launch traced here: 75.7 us
  Pallas kernels  66.9 us (88%)
  local copies, waits for them, and re-layouts  3.3 us (4%)
  between operations  3.06 us (4%)
  other arithmetic  2.43 us (3%)
    pallas_call x1, Pallas kernels, body(): pl.pallas_call(functools.partial(kernel, n_bits, n_z, n_mp, fuse, split),...  66.9 us
    slice x1, local copies, waits for them, and re-layouts, body(): out[p]  1.65 us
    concatenate x1, other arithmetic, body(): jnp.concatenate([out[p] for p in range(pieces // split - heads, pieces //...  1.58 us

profile of v2, /device:TPU:0, one launch (start us, length us, event | category | flops | bytes accessed | tf_op | source)
XLA Modules:
  0.0 75.7 jit_solution(15236719602035624860)
XLA Ops:
  1.3 66.9 %shard_map.111 = (f32[10,256,256]{2,1,0:T(8,128)}, f32[8,128]{1,0:T(8,128)}, f32[1,512]{1,0:T(1,128)}, f32[1,1]{1,0:T(1,128)}) custom-call(f32[256,512]{1,0:T(8,128)} %x_hbm.1, f32[256,512]{1,0:T(8,128)} %g_hbm.1, s32[1,256]{1,0:T(1,128)} %seg_hbm.1, s32[1,256]{1,0:T(1,128)} %bitcast.18, f32[512,1024]{1,0:T(8,128)} %w_hbm.1, f32[256,512]{1,0:T(8,128)} %wo_hbm.1, ...), custom_call_target="tpu_custom_call" | custom-call | tf_op jit(solution)/shard_map/pallas_call | solution.py:317
  68.2 1.1 %slice_bitcast_fusion.1 = (f32[256,256]{1,0:T(8,128)S(1)}, f32[256,256]{1,0:T(8,128)S(1)}) fusion(f32[5,512,256]{2,1,0:T(8,128)} %bitcast.13), kind=kLoop, calls=%fused_computation.3 | loop fusion | bytes 1048576 | tf_op jit(solution)/shard_map/squeeze | solution.py:378
  69.3 0.9 %pad_maximum_fusion.1 = f32[256,512]{1,0:T(8,128)} fusion(f32[256,256]{1,0:T(8,128)S(1)} %get-tuple-element.11, f32[256,256]{1,0:T(8,128)S(1)} %get-tuple-element.10), kind=kLoop, calls=%fused_computation.1 | loop fusion | flops 131072 | bytes 1048576 | tf_op jit(solution)/shard_map/concatenate | solution.py:378
  70.2 1.7 %fusion = (f32[2,256,256]{2,1,0:T(8,128)S(1)}, f32[2,256,256]{2,1,0:T(8,128)S(1)}, f32[2,256,256]{2,1,0:T(8,128)S(1)}, f32[2,256,256]{2,1,0:T(8,128)S(1)}) fusion(f32[10,256,256]{2,1,0:T(8,128)} %get-tuple-element.7), kind=kLoop, calls=%fused_computation.4 | loop fusion | bytes 4194304 | tf_op jit(solution)/shard_map/slice | solution.py:376
  71.8 0.0 copy-start
  71.8 1.6 %pad_maximum_fusion = f32[512,1024]{1,0:T(8,128)} fusion(f32[512,256]{1,0:T(8,128)S(1)} %bitcast.15, f32[512,256]{1,0:T(8,128)S(1)} %bitcast.16, f32[512,256]{1,0:T(8,128)S(1)} %bitcast.17, f32[512,256]{1,0:T(8,128)S(1)} %bitcast.14), kind=kLoop, calls=%fused_computation | loop fusion | flops 1572864 | bytes 4194304 | tf_op jit(solution)/shard_map/concatenate | solution.py:376
  73.4 0.0 copy-done
  73.4 0.6 copy.15
Async XLA Ops:
  71.8 1.6 %copy-start = (f32[1,512]{1,0:T(1,128)S(1)}, f32[1,512]{1,0:T(1,128)}, u32[]{:S(2)}) copy-start(f32[1,512]{1,0:T(1,128)} %get-tuple-element.22) | copy-start | bytes 6148

commit v3 on v1

v3 whole, which is shorter than its diff:
```python
import functools

import jax
import jax.numpy as jnp
from jax import lax
from jax.experimental import pallas as pl
from jax.experimental.pallas import tpu as pltpu
from jax.sharding import PartitionSpec as P

HEAD_DIM = 64
BLOCK = 4 * HEAD_DIM
MESH = pl.DeviceIdType.MESH
F32, BF16 = jnp.float32, jnp.bfloat16

NN = (((1,), (0,)), ((), ()))
NT = (((1,), (1,)), ((), ()))
TN = (((0,), (0,)), ((), ()))


def halves(value):
    high = value.astype(BF16)
    return high, (value - high.astype(F32)).astype(BF16)


def dot(left, right, dims):
    return lax.dot_general(left, right, dims, preferred_element_type=F32)


def dot3(left, right, dims):
    return dot(left[0], right[1], dims) + dot(left[1], right[0], dims) + dot(left[0], right[0], dims)


def remote(src, dst, send, recv, where):
    return pltpu.make_async_remote_copy(
        src_ref=src, dst_ref=dst, send_sem=send, recv_sem=recv, device_id=where, device_id_type=MESH
    )


def span(start, length):
    return pl.ds(pl.multiple_of(start, 8), length)


def compute_kernel(
    n_z, n_mp, fuse,
    x_hbm, g_hbm, seg_hbm, ids_hbm, w_hbm, wo_hbm,
    buf, sl, wopart_ref,
    x_ref, g_ref, seg_ref, ids_ref, w_ref, wo_ref, in_sem,
    xt_hi, xt_lo, act, dsilu, attn, dsfac, outv, dzs, stat, stat_in, ms, mr,
):
    loads = []
    for i, (src, dst) in enumerate((
        (seg_hbm, seg_ref), (x_hbm, x_ref), (w_hbm, w_ref), (g_hbm, g_ref),
        (wo_hbm, wo_ref), (ids_hbm, ids_ref),
    )):
        loads.append(pltpu.make_async_copy(src, dst, in_sem.at[i]))
        loads[-1].start()
    count, width = x_ref.shape
    heads = w_ref.shape[1] // BLOCK
    rows = sl.shape[0]
    off = 1 if fuse else 0
    scale = HEAD_DIM ** (-0.5)
    mp = lax.axis_index("mp")
    at_mp = [{"mp": lax.rem(mp + k, n_mp)} for k in range(1, n_mp)]
    own = rows // (n_z * 4 * n_mp)
    barrier = pltpu.get_barrier_semaphore()
    for partner in at_mp:
        pl.semaphore_signal(barrier, inc=1, device_id=partner, device_id_type=MESH)

    loads[0].wait()
    seg = jnp.broadcast_to(seg_ref[...].astype(F32), (count, count))
    spot = lax.broadcasted_iota(jnp.int32, (count, count), 0)
    other = lax.broadcasted_iota(jnp.int32, (count, count), 1)
    mask = jnp.where((seg == seg.T) & (spot >= other), 1.0, 0.0)
    loads[1].wait()
    xs = halves(x_ref[...])
    loads[3].wait()
    gs = halves(g_ref[...])
    loads[2].wait()
    loads[4].wait()

    def forward(h, sums):
        ws = halves(w_ref[:, pl.ds(pl.multiple_of(h * BLOCK, BLOCK), BLOCK)])
        pre = dot3(xs, ws, NN)
        sig = jax.nn.sigmoid(pre)
        val = pre * sig
        act[h] = val
        dsilu[h] = sig * (1.0 + pre * (1.0 - sig))
        u, v = val[:, 0:64], val[:, 64:128]
        q, k = val[:, 128:192], val[:, 192:256]
        score = dot3(halves(q), halves(k), NT) * scale
        ssig = jax.nn.sigmoid(score)
        a = score * ssig * mask
        attn[h] = a
        dsfac[h] = mask * (ssig * (1.0 + score * (1.0 - ssig))) * scale
        o = dot3(halves(a), halves(v), NN)
        outv[h] = o
        wos = halves(wo_ref[pl.ds(pl.multiple_of(h * HEAD_DIM, HEAD_DIM), HEAD_DIM), :])
        dz = dot3(gs, wos, NT)
        dzs[h] = dz
        dn = dz * u
        return (sums[0] + o, sums[1] + o * o, sums[2] + dn, sums[3] + dn * o)

    zero = jnp.zeros((count, HEAD_DIM), F32)
    sums = lax.fori_loop(0, heads, forward, (zero, zero, zero, zero))
    lane = lax.broadcasted_iota(jnp.int32, (count, 128), 1)
    packed = jnp.zeros((count, 128), F32)
    for i in range(4):
        packed = jnp.where(lane == i, jnp.sum(sums[i], axis=1, keepdims=True), packed)
    stat[...] = packed.T[0:8]
    pl.semaphore_wait(barrier, len(at_mp))

    def stat_to(k):
        return remote(stat, stat_in.at[k], ms.at[k], mr.at[k], at_mp[k])

    for k in range(n_mp - 1):
        stat_to(k).start()
    loads[5].wait()
    x_t = x_ref[...].T
    xt_hi[...], xt_lo[...] = halves(x_t)
    place = lax.broadcasted_iota(jnp.int32, (rows, count), 0)
    inner = n_z * n_mp * own
    pc, px = place // (2 * inner), (place // inner) % 2
    pz, pm = (place // (n_mp * own)) % n_z, place % (n_mp * own)
    wanted = ((pz * 2 + px) * 2 + pc) * (n_mp * own) + pm
    hits = jnp.where(wanted == ids_ref[...], 1.0, 0.0).astype(BF16)
    sl[...] = (dot(hits, gs[0], NN) + dot(hits, gs[1], NN)) * (1.0 / n_mp)

    total = stat[...]
    for k in range(n_mp - 1):
        stat_to(k).wait()
        total = total + stat_in[k]
    cols = jnp.concatenate([total, jnp.zeros((120, count), F32)], axis=0).T
    mean = cols[:, 0:1] / width
    var = cols[:, 1:2] / width - mean * mean
    rstd = lax.rsqrt(var + 1e-05)
    m1 = cols[:, 2:3] / width
    m2 = rstd * (cols[:, 3:4] - mean * cols[:, 2:3]) / width

    z_all = jnp.concatenate(
        [(outv[h] - mean) * rstd * act[h][:, 0:64] for h in range(heads)], axis=1
    )
    wo_grad = dot3(halves(z_all), gs, TN)
    if fuse:
        buf[0, 0:count] = wo_grad[:, 0:BLOCK]
        buf[0, count : 2 * count] = wo_grad[:, BLOCK : 2 * BLOCK]
        wopart_ref[...] = jnp.zeros(wopart_ref.shape, F32)
    else:
        wopart_ref[...] = wo_grad

    def backward(h, carry):
        val = act[h]
        u, v = val[:, 0:64], val[:, 64:128]
        q, k = val[:, 128:192], val[:, 192:256]
        nrm = (outv[h] - mean) * rstd
        dz = dzs[h]
        dn = dz * u
        du = dz * nrm
        do = halves(rstd * (dn - m1 - nrm * m2))
        da = dot3(do, halves(v), NT)
        dv = dot3(halves(attn[h]), do, TN)
        ds = halves(da * dsfac[h])
        dq = dot3(ds, halves(k), NN)
        dk = dot3(ds, halves(q), TN)
        dpre = halves(jnp.concatenate([du, dv, dq, dk], axis=1) * dsilu[h])
        buf[h + off] = dot3((xt_hi[...], xt_lo[...]), dpre, NN)
        rowsum = dot(hits, dpre[0], NN) + dot(hits, dpre[1], NN)
        ws = halves(w_ref[:, pl.ds(pl.multiple_of(h * BLOCK, BLOCK), BLOCK)])
        sl[...] += dot3(halves(rowsum), ws, NT)
        return carry

    lax.fori_loop(0, heads, backward, 0)


def sum_kernel(
    n_z, n_mp,
    part, sl, table_ref, accum_ref,
    out, newt_ref, newa_ref,
    acc, rc, rx, rz, sla, slc, slx, slz, slq, slm,
    ps, pr, zs, zr, ls, lr, lzs, lzr, ms, mr,
):
    pieces, width = part.shape[0], sl.shape[1]
    half = part.shape[1] // 2
    quarter = half // 2
    chunk = quarter // n_z
    rows, own = sl.shape[0], table_ref.shape[0]
    dp, mp = lax.axis_index("dp"), lax.axis_index("mp")
    z, x, c = dp // 4, (dp // 2) % 2, dp % 2
    at_core = {"dp": z * 4 + x * 2 + (1 - c)}
    at_x = {"dp": z * 4 + (1 - x) * 2 + c}
    z_of = [lax.rem(z + k, n_z) for k in range(1, n_z)]
    at_z = [{"dp": zz * 4 + x * 2 + c} for zz in z_of]
    at_mp = [{"mp": lax.rem(mp + k, n_mp)} for k in range(1, n_mp)]
    barrier = pltpu.get_barrier_semaphore()
    partners = [at_core, at_x] + at_z + at_mp
    for partner in partners:
        pl.semaphore_signal(barrier, inc=1, device_id=partner, device_id_type=MESH)
    pl.semaphore_wait(barrier, len(partners))

    mine = span(c * half, half)
    theirs = span((1 - c) * half, half)
    my_q, their_q = span(x * quarter, quarter), span((1 - x) * quarter, quarter)
    out_q = span(c * half + x * quarter, quarter)
    my_chunk = span(c * half + x * quarter + z * chunk, chunk)

    def core_rs(p):
        return remote(part.at[p, theirs], rc.at[p], ps.at[0, p], pr.at[0, p], at_core)

    def x_rs(p):
        return remote(acc.at[p, their_q], rx.at[p], ps.at[1, p], pr.at[1, p], at_x)

    def z_rs(p, k):
        there = span(x * quarter + z_of[k] * chunk, chunk)
        return remote(acc.at[p, there], rz.at[p, k], zs.at[0, p, k], zr.at[0, p, k], at_z[k])

    def z_ag(p, k):
        return remote(out.at[p, my_chunk], out.at[p, my_chunk], zs.at[1, p, k], zr.at[1, p, k], at_z[k])

    def x_ag(p):
        return remote(out.at[p, out_q], out.at[p, out_q], ps.at[2, p], pr.at[2, p], at_x)

    def core_ag(p):
        return remote(out.at[p, mine], out.at[p, mine], ps.at[3, p], pr.at[3, p], at_core)

    def stage(s, p):
        if s == 0:
            core_rs(p).start()
        elif s == 1:
            core_rs(p).wait()
            acc[p, their_q] = part[p, span(c * half + (1 - x) * quarter, quarter)] + rc[p, their_q]
            x_rs(p).start()
            acc[p, my_q] = part[p, out_q] + rc[p, my_q]
        elif s == 2:
            x_rs(p).wait()
            acc[p, my_q] += rx[p]
            for k in range(n_z - 1):
                z_rs(p, k).start()
        elif s == 3:
            total = acc[p, span(x * quarter + z * chunk, chunk)]
            for k in range(n_z - 1):
                z_rs(p, k).wait()
                total = total + rz[p, k]
            out[p, my_chunk] = total
            for k in range(n_z - 1):
                z_ag(p, k).start()
        elif s == 4:
            for k in range(n_z - 1):
                z_ag(p, k).wait()
            x_ag(p).start()
        elif s == 5:
            x_ag(p).wait()
            core_ag(p).start()
        else:
            core_ag(p).wait()

    s_half, s_q = rows // 2, rows // 4
    s_mine, s_theirs = span(x * s_q, s_q), span((1 - x) * s_q, s_q)

    def sl_core():
        return remote(sl.at[span((1 - c) * s_half, s_half)], slc, ls.at[0], lr.at[0], at_core)

    def sl_x():
        return remote(sla.at[s_theirs], slx, ls.at[1], lr.at[1], at_x)

    def sl_z(k):
        return remote(sla.at[s_mine], slz.at[k], lzs.at[k], lzr.at[k], at_z[k])

    def sl_mp(k):
        return remote(slq, slm.at[k], ms.at[k], mr.at[k], at_mp[k])

    def slab(t):
        if t == 0:
            sl_core().start()
        elif t == 1:
            sl_core().wait()
            sla[...] = sl[span(c * s_half, s_half)] + slc[...]
            sl_x().start()
        elif t == 2:
            sl_x().wait()
            sla[s_mine] += slx[...]
            for k in range(n_z - 1):
                sl_z(k).start()
        elif t == 3:
            row = sla[s_mine]
            for k in range(n_z - 1):
                sl_z(k).wait()
                row = row + slz[k]
            slq[...] = row
            for k in range(n_mp - 1):
                sl_mp(k).start()
        elif t == 4:
            row = slq[pl.ds((z * n_mp + mp) * own, own), :]
            for k in range(n_mp - 1):
                sl_mp(k).wait()
                row = row + slm[k, pl.ds((z * n_mp + mp) * own, own), :]
            newa = accum_ref[...] + jnp.sum(row * row, axis=1, keepdims=True) / width
            newa_ref[...] = newa
            newt_ref[...] = table_ref[...] - 0.5 * row * lax.rsqrt(newa)

    for s in range(7):
        for p in range(pieces):
            stage(s, p)
        if s <= 4:
            slab(s)


def body(layer_input, grad_out, segment, item_ids, w_uvqk, w_out, table, accum):
    count, width = layer_input.shape
    cols = w_uvqk.shape[1]
    heads = cols // BLOCK
    feats = heads * HEAD_DIM
    n_dp, n_mp = lax.axis_size("dp"), lax.axis_size("mp")
    own = table.shape[0]
    rows = own * n_dp * n_mp
    n_z = n_dp // 4
    fuse = feats == BLOCK and width // 2 // n_dp >= 8
    pieces = heads + (1 if fuse else 0)
    half, quarter = width // 2, width // 4
    chunk = quarter // n_z
    wo_shape = (8, 128) if fuse else (feats, width)
    vmem = pl.BlockSpec(memory_space=pltpu.VMEM)
    hbm = pl.BlockSpec(memory_space=pl.ANY)
    dma = pltpu.SemaphoreType.DMA
    parts, slab, wo_part = pl.pallas_call(
        functools.partial(compute_kernel, n_z, n_mp, fuse),
        out_shape=(
            jax.ShapeDtypeStruct((pieces, width, BLOCK), F32),
            jax.ShapeDtypeStruct((rows, width), F32),
            jax.ShapeDtypeStruct(wo_shape, F32),
        ),
        in_specs=[hbm] * 6,
        out_specs=(vmem,) * 3,
        scratch_shapes=[
            pltpu.VMEM((count, width), F32),
            pltpu.VMEM((count, width), F32),
            pltpu.VMEM((1, count), jnp.int32),
            pltpu.VMEM((1, count), jnp.int32),
            pltpu.VMEM((width, cols), F32),
            pltpu.VMEM((feats, width), F32),
            dma((6,)),
            pltpu.VMEM((width, count), BF16),
            pltpu.VMEM((width, count), BF16),
            pltpu.VMEM((heads, count, BLOCK), F32),
            pltpu.VMEM((heads, count, BLOCK), F32),
            pltpu.VMEM((heads, count, count), F32),
            pltpu.VMEM((heads, count, count), F32),
            pltpu.VMEM((heads, count, HEAD_DIM), F32),
            pltpu.VMEM((heads, count, HEAD_DIM), F32),
            pltpu.VMEM((8, count), F32),
            pltpu.VMEM((n_mp - 1, 8, count), F32),
            dma((n_mp - 1,)),
            dma((n_mp - 1,)),
        ],
        compiler_params=pltpu.CompilerParams(
            collective_id=0, has_side_effects=True, vmem_limit_bytes=56 * 1024 * 1024
        ),
    )(layer_input, grad_out, segment, item_ids.reshape(1, count), w_uvqk, w_out)
    out, new_table, new_accum = pl.pallas_call(
        functools.partial(sum_kernel, n_z, n_mp),
        out_shape=(
            jax.ShapeDtypeStruct((pieces, width, BLOCK), F32),
            jax.ShapeDtypeStruct((own, width), F32),
            jax.ShapeDtypeStruct((own, 1), F32),
        ),
        in_specs=[vmem] * 4,
        out_specs=(vmem,) * 3,
        scratch_shapes=[
            pltpu.VMEM((pieces, half, BLOCK), F32),
            pltpu.VMEM((pieces, half, BLOCK), F32),
            pltpu.VMEM((pieces, quarter, BLOCK), F32),
            pltpu.VMEM((pieces, n_z - 1, chunk, BLOCK), F32),
            pltpu.VMEM((rows // 2, width), F32),
            pltpu.VMEM((rows // 2, width), F32),
            pltpu.VMEM((rows // 4, width), F32),
            pltpu.VMEM((n_z - 1, rows // 4, width), F32),
            pltpu.VMEM((rows // 4, width), F32),
            pltpu.VMEM((n_mp - 1, rows // 4, width), F32),
            dma((4, pieces)),
            dma((4, pieces)),
            dma((2, pieces, n_z - 1)),
            dma((2, pieces, n_z - 1)),
            dma((2,)),
            dma((2,)),
            dma((n_z - 1,)),
            dma((n_z - 1,)),
            dma((n_mp - 1,)),
            dma((n_mp - 1,)),
        ],
        compiler_params=pltpu.CompilerParams(
            collective_id=1, has_side_effects=True, vmem_limit_bytes=30 * 1024 * 1024
        ),
    )(parts, slab, table, accum.reshape(own, 1))
    w_uvqk_grad = jnp.concatenate([out[p] for p in range(pieces - heads, pieces)], axis=1)
    if fuse:
        w_out_grad = jnp.concatenate([out[0, :feats], out[0, feats:]], axis=1)
    else:
        w_out_grad = lax.psum(wo_part, "dp")
    return w_uvqk_grad, w_out_grad, new_table, new_accum.reshape(own)


def solution(mesh):
    placed = (
        P("dp", None),
        P("dp", None),
        P("dp", None),
        P("dp"),
        P(None, "mp"),
        P("mp", None),
        P(("dp", "mp"), None),
        P(("dp", "mp")),
    )
    return jax.shard_map(
        body,
        mesh=mesh,
        in_specs=placed,
        out_specs=(P(None, "mp"), P("mp", None), P(("dp", "mp"), None), P(("dp", "mp"))),
        check_vma=False,
    )
```

time: 70 us -> 79.5 us (1.14)
  Pallas kernels: 56.6 us -> 70.1 us
  local copies, waits for them, and re-layouts: 7.5 us -> 3.33 us
    pallas_call x1 -> x2, Pallas kernels: 56.6 us -> 70.1 us  [the longest x1 50.3 us: body(): pl.pallas_call(functools.partial(sum_kernel, n_z, n_mp), out_shape=(jax.S...]
    unnamed x15 -> x7, local copies, waits for them, and re-layouts: 7.32 us -> 3.15 us
where the time goes in v3:
time: 79.5 us; the launch traced here: 79 us
  Pallas kernels  70.1 us (88%)
  local copies, waits for them, and re-layouts  3.33 us (4%)
  between operations  3.17 us (4%)
  other arithmetic  2.43 us (3%)
    pallas_call x1, Pallas kernels, body(): pl.pallas_call(functools.partial(sum_kernel, n_z, n_mp), out_shape=(jax.S...  50.3 us
    pallas_call x1, Pallas kernels, body(): pl.pallas_call(functools.partial(compute_kernel, n_z, n_mp, fuse), out_sh...  19.8 us
    unnamed x7, local copies, waits for them, and re-layouts  3.15 us

profile of v3, /device:TPU:0, one launch (start us, length us, event | category | flops | bytes accessed | tf_op | source)
XLA Modules:
  0.0 79.0 jit_solution(11676199944064567015)
XLA Ops:
  0.6 0.0 copy-start.2
  1.3 19.8 %shard_map.111 = (f32[5,512,256]{2,1,0:T(8,128)}, f32[32,512]{1,0:T(8,128)}, f32[8,128]{1,0:T(8,128)}) custom-call(f32[256,512]{1,0:T(8,128)} %x_hbm.1, f32[256,512]{1,0:T(8,128)} %g_hbm.1, s32[1,256]{1,0:T(1,128)} %seg_hbm.1, s32[1,256]{1,0:T(1,128)} %bitcast.16, f32[512,1024]{1,0:T(8,128)} %w_hbm.1, f32[256,512]{1,0:T(8,128)} %wo_hbm.1), custom_call_target="tpu_custom_call" | custom-call | tf_op jit(solution)/shard_map/pallas_call | solution.py:323
  21.1 0.0 copy-done.2
  21.1 0.0 copy-start
  21.1 1.7 %copy-done = f32[5,512,256]{2,1,0:T(8,128)S(1)} copy-done((f32[5,512,256]{2,1,0:T(8,128)S(1)}, f32[5,512,256]{2,1,0:T(8,128)}, u32[]{:S(2)}) %copy-start) | copy-done | bytes 2621464
  22.9 0.0 copy-start.1
  22.9 0.8 %copy-done.1 = f32[32,512]{1,0:T(8,128)S(1)} copy-done((f32[32,512]{1,0:T(8,128)S(1)}, f32[32,512]{1,0:T(8,128)}, u32[]{:S(2)}) %copy-start.1) | copy-done | bytes 65560
  23.7 50.3 %shard_map.112 = (f32[5,512,256]{2,1,0:T(8,128)S(1)}, f32[1,512]{1,0:T(1,128)S(1)}, f32[1,1]{1,0:T(1,128)}) custom-call(f32[5,512,256]{2,1,0:T(8,128)S(1)} %copy-done, f32[32,512]{1,0:T(8,128)S(1)} %copy-done.1, f32[1,512]{1,0:T(1,128)S(1)} %copy-done.2, f32[1,1]{1,0:T(1,128)} %bitcast.15.accum_ref), custom_call_target="tpu_custom_call" | custom-call | tf_op jit(solution)/shard_map/pallas_call | solution.py:357
  74.0 0.1 slice_bitcast_fusion.3
  74.2 1.6 %pad_maximum_fusion = f32[512,1024]{1,0:T(8,128)} fusion(f32[512,256]{1,0:T(8,128)S(1)} %get-tuple-element.17, f32[512,256]{1,0:T(8,128)S(1)} %get-tuple-element.18, f32[512,256]{1,0:T(8,128)S(1)} %get-tuple-element.19, f32[512,256]{1,0:T(8,128)S(1)} %get-tuple-element.16), kind=kLoop, calls=%fused_computation | loop fusion | flops 1572864 | bytes 4194304 | tf_op jit(solution)/shard_map/concatenate | solution.py:392
  75.8 0.9 %pad_maximum_fusion.1 = f32[256,512]{1,0:T(8,128)} fusion(f32[256,256]{1,0:T(8,128)S(1)} %get-tuple-element.15, f32[256,256]{1,0:T(8,128)S(1)} %get-tuple-element.14), kind=kLoop, calls=%fused_computation.1 | loop fusion | flops 131072 | bytes 1048576 | tf_op jit(solution)/shard_map/concatenate | solution.py:394
  76.6 0.6 copy.15
  (1 shorter events, 0.0 us)
Async XLA Ops:
  0.6 20.5 %copy-start.2 = (f32[1,512]{1,0:T(1,128)S(1)}, f32[1,512]{1,0:T(1,128)}, u32[]{:S(2)}) copy-start(f32[1,512]{1,0:T(1,128)} %table_ref.1) | copy-start | bytes 6148
  21.1 1.7 %copy-start = (f32[5,512,256]{2,1,0:T(8,128)S(1)}, f32[5,512,256]{2,1,0:T(8,128)}, u32[]{:S(2)}) copy-start(f32[5,512,256]{2,1,0:T(8,128)} %get-tuple-element.9.part) | copy-start | bytes 7864324
  22.9 0.8 %copy-start.1 = (f32[32,512]{1,0:T(8,128)S(1)}, f32[32,512]{1,0:T(8,128)}, u32[]{:S(2)}) copy-start(f32[32,512]{1,0:T(8,128)} %get-tuple-element.10.sl) | copy-start | bytes 196612

commit v4 on v1

--- a/solution.py
+++ b/solution.py
@@ -32,12 +32,20 @@
 
 def kernel(
     n_z, n_mp, fuse,
-    x_ref, g_ref, seg_ref, ids_ref, w_ref, wo_ref, table_ref, accum_ref,
-    out, wopart_ref, newt_ref, newa_ref,
-    buf, xt_hi, xt_lo, act, dsilu, attn, dsfac, outv, dzs, stat, stat_in,
+    x_hbm, g_hbm, seg_hbm, ids_hbm, w_hbm, wo_hbm, table_hbm, accum_ref,
+    out_hbm, wopart_ref, newt_ref, newa_ref,
+    x_ref, g_ref, seg_ref, ids_ref, w_ref, wo_ref, table_ref, in_sem, out_sem,
+    out, buf, xt_hi, xt_lo, act, dsilu, attn, dsfac, outv, dzs, stat, stat_in,
     rc, rx, rz, sl, slc, slx, slz, slq, slm,
     ps, pr, zs, zr, ls, lr, lzs, lzr, ms, mr,
 ):
+    loads = []
+    for i, (src, dst) in enumerate((
+        (seg_hbm, seg_ref), (x_hbm, x_ref), (w_hbm, w_ref), (g_hbm, g_ref),
+        (wo_hbm, wo_ref), (ids_hbm, ids_ref), (table_hbm, table_ref),
+    )):
+        loads.append(pltpu.make_async_copy(src, dst, in_sem.at[i]))
+        loads[-1].start()
     count, width = x_ref.shape
     heads = w_ref.shape[1] // BLOCK
     rows = sl.shape[0]
@@ -94,6 +102,9 @@
 
     def core_ag(p):
         return remote(out.at[p, mine], out.at[p, mine], ps.at[3, p], pr.at[3, p], at_core)
+
+    def keep(p):
+        return pltpu.make_async_copy(out.at[p], out_hbm.at[p], out_sem.at[p])
 
     def stage(s, p):
         if s == 0:
@@ -125,13 +136,19 @@
             core_ag(p).start()
         else:
             core_ag(p).wait()
-
+            keep(p).start()
+
+    loads[0].wait()
     seg = jnp.broadcast_to(seg_ref[...].astype(F32), (count, count))
     spot = lax.broadcasted_iota(jnp.int32, (count, count), 0)
     other = lax.broadcasted_iota(jnp.int32, (count, count), 1)
     mask = jnp.where((seg == seg.T) & (spot >= other), 1.0, 0.0)
+    loads[1].wait()
     xs = halves(x_ref[...])
+    loads[3].wait()
     gs = halves(g_ref[...])
+    loads[2].wait()
+    loads[4].wait()
 
     def forward(h, sums):
         ws = halves(w_ref[:, pl.ds(pl.multiple_of(h * BLOCK, BLOCK), BLOCK)])
@@ -169,6 +186,8 @@
 
     for k in range(n_mp - 1):
         stat_to(k).start()
+    loads[5].wait()
+    loads[6].wait()
     x_t = x_ref[...].T
     xt_hi[...], xt_lo[...] = halves(x_t)
     place = lax.broadcasted_iota(jnp.int32, (rows, count), 0)
@@ -282,6 +301,26 @@
             if 0 <= tick - s < pieces:
                 stage(s, tick - s)
         slab(t)
+    for p in range(pieces):
+        keep(p).wait()
+
+
+def layout_kernel(off, pieces_ref, table_ref, *refs):
+    sem = refs[-1]
+    w_ref, newt_ref = refs[0], refs[1]
+    moves = [(table_ref, newt_ref)]
+    for h in range(w_ref.shape[1] // BLOCK):
+        moves.append((pieces_ref.at[h + off], w_ref.at[:, pl.ds(h * BLOCK, BLOCK)]))
+    if off:
+        wo_ref = refs[2]
+        count = wo_ref.shape[0]
+        for i in range(2):
+            moves.append((pieces_ref.at[0, pl.ds(i * count, count)], wo_ref.at[:, pl.ds(i * BLOCK, BLOCK)]))
+    copies = [pltpu.make_async_copy(src, dst, sem.at[i]) for i, (src, dst) in enumerate(moves)]
+    for copy in copies:
+        copy.start()
+    for copy in copies:
+        copy.wait()
 
 
 def body(layer_input, grad_out, segment, item_ids, w_uvqk, w_out, table, accum):
@@ -293,12 +332,13 @@
     own = table.shape[0]
     rows = own * n_dp * n_mp
     n_z = n_dp // 4
-    fuse = feats * width == width * BLOCK
+    fuse = feats == BLOCK
     pieces = heads + (1 if fuse else 0)
     half, quarter = width // 2, width // 4
     chunk = quarter // n_z
     wo_shape = (8, 128) if fuse else (feats, width)
     vmem = pl.BlockSpec(memory_space=pltpu.VMEM)
+    hbm = pl.BlockSpec(memory_space=pl.ANY)
     dma = pltpu.SemaphoreType.DMA
     out, wo_part, new_table, new_accum = pl.pallas_call(
         functools.partial(kernel, n_z, n_mp, fuse),
@@ -308,9 +348,19 @@
             jax.ShapeDtypeStruct((own, width), F32),
             jax.ShapeDtypeStruct((own, 1), F32),
         ),
-        in_specs=[vmem] * 8,
-        out_specs=(vmem,) * 4,
+        in_specs=[hbm] * 7 + [vmem],
+        out_specs=(hbm, vmem, vmem, vmem),
         scratch_shapes=[
+            pltpu.VMEM((count, width), F32),
+            pltpu.VMEM((count, width), F32),
+            pltpu.VMEM((1, count), jnp.int32),
+            pltpu.VMEM((1, count), jnp.int32),
+            pltpu.VMEM((width, cols), F32),
+            pltpu.VMEM((feats, width), F32),
+            pltpu.VMEM((own, width), F32),
+            dma((7,)),
+            dma((pieces,)),
+            pltpu.VMEM((pieces, width, BLOCK), F32),
             pltpu.VMEM((pieces, width, BLOCK), F32),
             pltpu.VMEM((width, count), BF16),
             pltpu.VMEM((width, count), BF16),
@@ -343,7 +393,7 @@
             dma((2, n_mp - 1)),
         ],
         compiler_params=pltpu.CompilerParams(
-            collective_id=0, has_side_effects=True, vmem_limit_bytes=40 * 1024 * 1024
+            collective_id=0, has_side_effects=True, vmem_limit_bytes=56 * 1024 * 1024
         ),
     )(
         layer_input,
@@ -355,11 +405,20 @@
         table,
         accum.reshape(own, 1),
     )
-    w_uvqk_grad = jnp.concatenate([out[p] for p in range(pieces - heads, pieces)], axis=1)
-    if fuse:
-        w_out_grad = jnp.concatenate([out[0, :feats], out[0, feats:]], axis=1)
-    else:
-        w_out_grad = lax.psum(wo_part, "dp")
+    results = [
+        jax.ShapeDtypeStruct((width, cols), F32),
+        jax.ShapeDtypeStruct((own, width), F32),
+    ] + ([jax.ShapeDtypeStruct((feats, width), F32)] if fuse else [])
+    laid = pl.pallas_call(
+        functools.partial(layout_kernel, 1 if fuse else 0),
+        out_shape=tuple(results),
+        in_specs=[hbm] * 2,
+        out_specs=(hbm,) * len(results),
+        scratch_shapes=[dma((heads + 3,))],
+        compiler_params=pltpu.CompilerParams(vmem_limit_bytes=56 * 1024 * 1024),
+    )(out, new_table)
+    w_uvqk_grad, new_table = laid[:2]
+    w_out_grad = laid[2] if fuse else lax.psum(wo_part, "dp")
     return w_uvqk_grad, w_out_grad, new_table, new_accum.reshape(own)
 
 

time: 70 us -> 143 us (2.04)
  Pallas kernels: 56.6 us -> 140 us
  local copies, waits for them, and re-layouts: 7.5 us -> 0 us
  other arithmetic: 2.43 us -> 0 us
    pallas_call x0 -> x1, Pallas kernels: none -> 80.6 us  [body(): pl.pallas_call(functools.partial(layout_kernel, 1 if fuse else 0), out_sh...]
    unnamed x15 -> x0, local copies, waits for them, and re-layouts: 7.32 us -> none
    pallas_call x1, Pallas kernels: 56.6 us -> 59.3 us  [body(): pl.pallas_call(functools.partial(kernel, n_z, n_mp, fuse), out_shape=(jax...]
    concatenate x2 -> x0, other arithmetic: 2.43 us -> none  [the longest x1 1.58 us: body(): jnp.concatenate([out[p] for p in range(pieces - heads, pieces)], axis=1)]
where the time goes in v4:
time: 143 us
  Pallas kernels  140 us (98%)
  between operations  3.11 us (2%)
    pallas_call x1, Pallas kernels, body(): pl.pallas_call(functools.partial(layout_kernel, 1 if fuse else 0), out_sh...  80.6 us
    pallas_call x1, Pallas kernels, body(): pl.pallas_call(functools.partial(kernel, n_z, n_mp, fuse), out_shape=(jax...  59.3 us

profile of v4, /device:TPU:0, one launch (start us, length us, event | category | flops | bytes accessed | tf_op | source)
XLA Modules:
  0.0 143.0 jit_solution(12562673122171718132)
XLA Ops:
  1.3 59.3 %shard_map.111 = (f32[5,512,256]{2,1,0:T(8,128)}, f32[8,128]{1,0:T(8,128)}, f32[1,512]{1,0:T(1,128)}, f32[1,1]{1,0:T(1,128)}) custom-call(f32[256,512]{1,0:T(8,128)} %x_hbm.1, f32[256,512]{1,0:T(8,128)} %g_hbm.1, s32[1,256]{1,0:T(1,128)} %seg_hbm.1, s32[1,256]{1,0:T(1,128)} %bitcast.4, f32[512,1024]{1,0:T(8,128)} %w_hbm.1, f32[256,512]{1,0:T(8,128)} %wo_hbm.1, ...), custom_call_target="tpu_custom_call" | custom-call | tf_op jit(solution)/shard_map/pallas_call | solution.py:343
  60.6 80.6 %shard_map.112 = (f32[512,1024]{1,0:T(8,128)}, f32[1,512]{1,0:T(1,128)}, f32[256,512]{1,0:T(8,128)}) custom-call(f32[5,512,256]{2,1,0:T(8,128)} %get-tuple-element.10.pieces_ref, f32[1,512]{1,0:T(1,128)} %get-tuple-element.11.table_ref), custom_call_target="tpu_custom_call" | custom-call | tf_op jit(solution)/shard_map/pallas_call | solution.py:412

commit v5 on v4

--- a/solution.py
+++ b/solution.py
@@ -306,19 +306,29 @@
 
 
 def layout_kernel(off, pieces_ref, table_ref, *refs):
-    sem = refs[-1]
+    held, row, in_sem, sem = refs[-4:]
     w_ref, newt_ref = refs[0], refs[1]
-    moves = [(table_ref, newt_ref)]
-    for h in range(w_ref.shape[1] // BLOCK):
-        moves.append((pieces_ref.at[h + off], w_ref.at[:, pl.ds(h * BLOCK, BLOCK)]))
-    if off:
-        wo_ref = refs[2]
-        count = wo_ref.shape[0]
-        for i in range(2):
-            moves.append((pieces_ref.at[0, pl.ds(i * count, count)], wo_ref.at[:, pl.ds(i * BLOCK, BLOCK)]))
-    copies = [pltpu.make_async_copy(src, dst, sem.at[i]) for i, (src, dst) in enumerate(moves)]
-    for copy in copies:
-        copy.start()
+    count = held.shape[0]
+    loads = [pltpu.make_async_copy(pieces_ref.at[p], held.at[p], in_sem.at[p]) for p in range(count)]
+    loads.append(pltpu.make_async_copy(table_ref, row, in_sem.at[count]))
+    for load in loads:
+        load.start()
+    moves = []
+    for p in range(count):
+        if p < off:
+            tokens = refs[2].shape[0]
+            moves.append([
+                (held.at[p, pl.ds(i * tokens, tokens)], refs[2].at[:, pl.ds(i * BLOCK, BLOCK)]) for i in range(2)
+            ])
+        else:
+            moves.append([(held.at[p], w_ref.at[:, pl.ds((p - off) * BLOCK, BLOCK)])])
+    moves.append([(row, newt_ref)])
+    copies = []
+    for load, after in zip(loads, moves):
+        load.wait()
+        for src, dst in after:
+            copies.append(pltpu.make_async_copy(src, dst, sem.at[len(copies)]))
+            copies[-1].start()
     for copy in copies:
         copy.wait()
 
@@ -414,7 +424,12 @@
         out_shape=tuple(results),
         in_specs=[hbm] * 2,
         out_specs=(hbm,) * len(results),
-        scratch_shapes=[dma((heads + 3,))],
+        scratch_shapes=[
+            pltpu.VMEM((pieces, width, BLOCK), F32),
+            pltpu.VMEM((own, width), F32),
+            dma((pieces + 1,)),
+            dma((heads + 3,)),
+        ],
         compiler_params=pltpu.CompilerParams(vmem_limit_bytes=56 * 1024 * 1024),
     )(out, new_table)
     w_uvqk_grad, new_table = laid[:2]

time: 143 us -> 65.2 us (0.46)
  Pallas kernels: 140 us -> 61.9 us
    pallas_call x1, Pallas kernels: 80.6 us -> 2.64 us  [body(): pl.pallas_call(functools.partial(layout_kernel, 1 if fuse else 0), out_sh...]
where the time goes in v5:
time: 65.2 us; the launch traced here: 65 us
  Pallas kernels  61.9 us (95%)
  between operations  3.11 us (5%)
    pallas_call x1, Pallas kernels, body(): pl.pallas_call(functools.partial(kernel, n_z, n_mp, fuse), out_shape=(jax...  59.3 us
    pallas_call x1, Pallas kernels, body(): pl.pallas_call(functools.partial(layout_kernel, 1 if fuse else 0), out_sh...  2.64 us

profile of v5, /device:TPU:0, one launch (start us, length us, event | category | flops | bytes accessed | tf_op | source)
XLA Modules:
  0.0 65.0 jit_solution(6542642725861695504)
XLA Ops:
  1.3 59.3 %shard_map.111 = (f32[5,512,256]{2,1,0:T(8,128)}, f32[8,128]{1,0:T(8,128)}, f32[1,512]{1,0:T(1,128)}, f32[1,1]{1,0:T(1,128)}) custom-call(f32[256,512]{1,0:T(8,128)} %x_hbm.1, f32[256,512]{1,0:T(8,128)} %g_hbm.1, s32[1,256]{1,0:T(1,128)} %seg_hbm.1, s32[1,256]{1,0:T(1,128)} %bitcast.4, f32[512,1024]{1,0:T(8,128)} %w_hbm.1, f32[256,512]{1,0:T(8,128)} %wo_hbm.1, ...), custom_call_target="tpu_custom_call" | custom-call | tf_op jit(solution)/shard_map/pallas_call | solution.py:353
  60.6 2.6 %shard_map.112 = (f32[512,1024]{1,0:T(8,128)}, f32[1,512]{1,0:T(1,128)}, f32[256,512]{1,0:T(8,128)}) custom-call(f32[5,512,256]{2,1,0:T(8,128)} %get-tuple-element.10.pieces_ref, f32[1,512]{1,0:T(1,128)} %get-tuple-element.11.table_ref), custom_call_target="tpu_custom_call" | custom-call | tf_op jit(solution)/shard_map/pallas_call | solution.py:422

commit v6 on v5

--- a/solution.py
+++ b/solution.py
@@ -39,15 +39,18 @@
     rc, rx, rz, sl, slc, slx, slz, slq, slm,
     ps, pr, zs, zr, ls, lr, lzs, lzr, ms, mr,
 ):
-    loads = []
-    for i, (src, dst) in enumerate((
-        (seg_hbm, seg_ref), (x_hbm, x_ref), (w_hbm, w_ref), (g_hbm, g_ref),
-        (wo_hbm, wo_ref), (ids_hbm, ids_ref), (table_hbm, table_ref),
-    )):
-        loads.append(pltpu.make_async_copy(src, dst, in_sem.at[i]))
-        loads[-1].start()
     count, width = x_ref.shape
     heads = w_ref.shape[1] // BLOCK
+    moves = [(seg_hbm, seg_ref), (x_hbm, x_ref)]
+    for h in range(heads):
+        at = pl.ds(h * BLOCK, BLOCK)
+        moves.append((w_hbm.at[:, at], w_ref.at[:, at]))
+    moves += [(g_hbm, g_ref), (wo_hbm, wo_ref), (ids_hbm, ids_ref), (table_hbm, table_ref)]
+    loads = [pltpu.make_async_copy(src, dst, in_sem.at[i]) for i, (src, dst) in enumerate(moves)]
+    for load in loads:
+        load.start()
+    w_loads = loads[2 : 2 + heads]
+    loads = loads[:2] + loads[2 + heads :]
     rows = sl.shape[0]
     own = table_ref.shape[0]
     off = 1 if fuse else 0
@@ -145,13 +148,13 @@
     mask = jnp.where((seg == seg.T) & (spot >= other), 1.0, 0.0)
     loads[1].wait()
     xs = halves(x_ref[...])
+    loads[2].wait()
+    gs = halves(g_ref[...])
     loads[3].wait()
-    gs = halves(g_ref[...])
-    loads[2].wait()
-    loads[4].wait()
 
     def forward(h, sums):
-        ws = halves(w_ref[:, pl.ds(pl.multiple_of(h * BLOCK, BLOCK), BLOCK)])
+        w_loads[h].wait()
+        ws = halves(w_ref[:, h * BLOCK : (h + 1) * BLOCK])
         pre = dot3(xs, ws, NN)
         sig = jax.nn.sigmoid(pre)
         val = pre * sig
@@ -166,14 +169,16 @@
         dsfac[h] = mask * (ssig * (1.0 + score * (1.0 - ssig))) * scale
         o = dot3(halves(a), halves(v), NN)
         outv[h] = o
-        wos = halves(wo_ref[pl.ds(pl.multiple_of(h * HEAD_DIM, HEAD_DIM), HEAD_DIM), :])
+        wos = halves(wo_ref[h * HEAD_DIM : (h + 1) * HEAD_DIM, :])
         dz = dot3(gs, wos, NT)
         dzs[h] = dz
         dn = dz * u
         return (sums[0] + o, sums[1] + o * o, sums[2] + dn, sums[3] + dn * o)
 
     zero = jnp.zeros((count, HEAD_DIM), F32)
-    sums = lax.fori_loop(0, heads, forward, (zero, zero, zero, zero))
+    sums = (zero, zero, zero, zero)
+    for h in range(heads):
+        sums = forward(h, sums)
     lane = lax.broadcasted_iota(jnp.int32, (count, 128), 1)
     packed = jnp.zeros((count, 128), F32)
     for i in range(4):
@@ -186,8 +191,8 @@
 
     for k in range(n_mp - 1):
         stat_to(k).start()
+    loads[4].wait()
     loads[5].wait()
-    loads[6].wait()
     x_t = x_ref[...].T
     xt_hi[...], xt_lo[...] = halves(x_t)
     place = lax.broadcasted_iota(jnp.int32, (rows, count), 0)
@@ -368,7 +373,7 @@
             pltpu.VMEM((width, cols), F32),
             pltpu.VMEM((feats, width), F32),
             pltpu.VMEM((own, width), F32),
-            dma((7,)),
+            dma((heads + 6,)),
             dma((pieces,)),
             pltpu.VMEM((pieces, width, BLOCK), F32),
             pltpu.VMEM((pieces, width, BLOCK), F32),

time: 65.2 us -> 66.2 us (1.015)
  Pallas kernels: 61.9 us -> 62.9 us
    pallas_call x1, Pallas kernels: 59.3 us -> 60.2 us  [body(): pl.pallas_call(functools.partial(kernel, n_z, n_mp, fuse), out_shape=(jax...]
where the time goes in v6:
time: 66.2 us; the launch traced here: 66 us
  Pallas kernels  62.9 us (95%)
  between operations  3.11 us (5%)
    pallas_call x1, Pallas kernels, body(): pl.pallas_call(functools.partial(kernel, n_z, n_mp, fuse), out_shape=(jax...  60.2 us
    pallas_call x1, Pallas kernels, body(): pl.pallas_call(functools.partial(layout_kernel, 1 if fuse else 0), out_sh...  2.64 us

profile of v6, /device:TPU:0, one launch (start us, length us, event | category | flops | bytes accessed | tf_op | source)
XLA Modules:
  0.0 66.0 jit_solution(1694279745201545129)
XLA Ops:
  1.3 60.2 %shard_map.111 = (f32[5,512,256]{2,1,0:T(8,128)}, f32[8,128]{1,0:T(8,128)}, f32[1,512]{1,0:T(1,128)}, f32[1,1]{1,0:T(1,128)}) custom-call(f32[256,512]{1,0:T(8,128)} %x_hbm.1, f32[256,512]{1,0:T(8,128)} %g_hbm.1, s32[1,256]{1,0:T(1,128)} %seg_hbm.1, s32[1,256]{1,0:T(1,128)} %bitcast.4, f32[512,1024]{1,0:T(8,128)} %w_hbm.1, f32[256,512]{1,0:T(8,128)} %wo_hbm.1, ...), custom_call_target="tpu_custom_call" | custom-call | tf_op jit(solution)/shard_map/pallas_call | solution.py:358
  61.5 2.6 %shard_map.112 = (f32[512,1024]{1,0:T(8,128)}, f32[1,512]{1,0:T(1,128)}, f32[256,512]{1,0:T(8,128)}) custom-call(f32[5,512,256]{2,1,0:T(8,128)} %get-tuple-element.10.pieces_ref, f32[1,512]{1,0:T(1,128)} %get-tuple-element.11.table_ref), custom_call_target="tpu_custom_call" | custom-call | tf_op jit(solution)/shard_map/pallas_call | solution.py:427

commit v7 on v5

--- a/solution.py
+++ b/solution.py
@@ -9,6 +9,7 @@
 
 HEAD_DIM = 64
 BLOCK = 4 * HEAD_DIM
+ORDER = (0, 1, 3, 4, 2, 5, 6)
 MESH = pl.DeviceIdType.MESH
 F32, BF16 = jnp.float32, jnp.bfloat16
 
@@ -241,7 +242,7 @@
         rowsum = dot(hits, dpre[0], NN) + dot(hits, dpre[1], NN)
         ws = halves(w_ref[:, pl.ds(pl.multiple_of(h * BLOCK, BLOCK), BLOCK)])
         sl[...] += dot3(halves(rowsum), ws, NT)
-        for s in range(1, min(6, heads - 1 + off) + 1):
+        for s in [s for s in ORDER if 1 <= s <= heads - 1 + off]:
             if off == 1 and s == 1:
                 stage(s, h)
             else:
@@ -297,7 +298,7 @@
     slab(0)
     for t in range(1, 7):
         tick = heads - 1 + off + t
-        for s in range(0, 7):
+        for s in ORDER:
             if 0 <= tick - s < pieces:
                 stage(s, tick - s)
         slab(t)

time: 65.2 us -> 71.2 us (1.092)
  Pallas kernels: 61.9 us -> 67.9 us
    pallas_call x1, Pallas kernels: 59.3 us -> 65.3 us  [body(): pl.pallas_call(functools.partial(kernel, n_z, n_mp, fuse), out_shape=(jax...]
where the time goes in v7:
time: 71.2 us; the launch traced here: 71 us
  Pallas kernels  67.9 us (95%)
  between operations  3.11 us (4%)
    pallas_call x1, Pallas kernels, body(): pl.pallas_call(functools.partial(kernel, n_z, n_mp, fuse), out_shape=(jax...  65.3 us
    pallas_call x1, Pallas kernels, body(): pl.pallas_call(functools.partial(layout_kernel, 1 if fuse else 0), out_sh...  2.64 us

profile of v7, /device:TPU:0, one launch (start us, length us, event | category | flops | bytes accessed | tf_op | source)
XLA Modules:
  0.0 71.0 jit_solution(11422451432122645811)
XLA Ops:
  1.3 65.3 %shard_map.111 = (f32[5,512,256]{2,1,0:T(8,128)}, f32[8,128]{1,0:T(8,128)}, f32[1,512]{1,0:T(1,128)}, f32[1,1]{1,0:T(1,128)}) custom-call(f32[256,512]{1,0:T(8,128)} %x_hbm.1, f32[256,512]{1,0:T(8,128)} %g_hbm.1, s32[1,256]{1,0:T(1,128)} %seg_hbm.1, s32[1,256]{1,0:T(1,128)} %bitcast.4, f32[512,1024]{1,0:T(8,128)} %w_hbm.1, f32[256,512]{1,0:T(8,128)} %wo_hbm.1, ...), custom_call_target="tpu_custom_call" | custom-call | tf_op jit(solution)/shard_map/pallas_call | solution.py:354
  66.5 2.6 %shard_map.112 = (f32[512,1024]{1,0:T(8,128)}, f32[1,512]{1,0:T(1,128)}, f32[256,512]{1,0:T(8,128)}) custom-call(f32[5,512,256]{2,1,0:T(8,128)} %get-tuple-element.10.pieces_ref, f32[1,512]{1,0:T(1,128)} %get-tuple-element.11.table_ref), custom_call_target="tpu_custom_call" | custom-call | tf_op jit(solution)/shard_map/pallas_call | solution.py:423

commit v8 on v5

--- a/solution.py
+++ b/solution.py
@@ -37,7 +37,7 @@
     x_ref, g_ref, seg_ref, ids_ref, w_ref, wo_ref, table_ref, in_sem, out_sem,
     out, buf, xt_hi, xt_lo, act, dsilu, attn, dsfac, outv, dzs, stat, stat_in,
     rc, rx, rz, sl, slc, slx, slz, slq, slm,
-    ps, pr, zs, zr, ls, lr, lzs, lzr, ms, mr,
+    ps, pr, x_send, x_recv, zs, zr, ls, lr, lzs, lzr, ms, mr,
 ):
     loads = []
     for i, (src, dst) in enumerate((
@@ -97,8 +97,9 @@
     def z_ag(p, k):
         return remote(out.at[p, my_chunk], out.at[p, my_chunk], zs.at[1, p, k], zr.at[1, p, k], at_z[k])
 
-    def x_ag(p):
-        return remote(out.at[p, my_q], out.at[p, my_q], ps.at[2, p], pr.at[2, p], at_x)
+    def x_ag(p, k):
+        at = span(c * half + x * quarter + lax.rem(z - k + n_z, n_z) * chunk, chunk)
+        return remote(out.at[p, at], out.at[p, at], x_send.at[p, k], x_recv.at[p, k], at_x)
 
     def core_ag(p):
         return remote(out.at[p, mine], out.at[p, mine], ps.at[3, p], pr.at[3, p], at_core)
@@ -127,12 +128,14 @@
             out[p, my_chunk] = total
             for k in range(n_z - 1):
                 z_ag(p, k).start()
+            x_ag(p, 0).start()
         elif s == 4:
             for k in range(n_z - 1):
                 z_ag(p, k).wait()
-            x_ag(p).start()
+                x_ag(p, k + 1).start()
         elif s == 5:
-            x_ag(p).wait()
+            for k in range(n_z):
+                x_ag(p, k).wait()
             core_ag(p).start()
         else:
             core_ag(p).wait()
@@ -393,6 +396,8 @@
             pltpu.VMEM((n_mp - 1, rows // 4, width), F32),
             dma((4, pieces)),
             dma((4, pieces)),
+            dma((pieces, n_z)),
+            dma((pieces, n_z)),
             dma((2, pieces, n_z - 1)),
             dma((2, pieces, n_z - 1)),
             dma((2,)),

time: 65.2 us -> 64.7 us (level)
  no operation moved by 1% of the time
where the time goes in v8:
time: 64.7 us; the launch traced here: 64.5 us
  Pallas kernels  61.4 us (95%)
  between operations  3.11 us (5%)
    pallas_call x1, Pallas kernels, body(): pl.pallas_call(functools.partial(kernel, n_z, n_mp, fuse), out_shape=(jax...  58.8 us
    pallas_call x1, Pallas kernels, body(): pl.pallas_call(functools.partial(layout_kernel, 1 if fuse else 0), out_sh...  2.64 us

profile of v8, /device:TPU:0, one launch (start us, length us, event | category | flops | bytes accessed | tf_op | source)
XLA Modules:
  0.0 64.5 jit_solution(1429368545045371098)
XLA Ops:
  1.3 58.8 %shard_map.111 = (f32[5,512,256]{2,1,0:T(8,128)}, f32[8,128]{1,0:T(8,128)}, f32[1,512]{1,0:T(1,128)}, f32[1,1]{1,0:T(1,128)}) custom-call(f32[256,512]{1,0:T(8,128)} %x_hbm.1, f32[256,512]{1,0:T(8,128)} %g_hbm.1, s32[1,256]{1,0:T(1,128)} %seg_hbm.1, s32[1,256]{1,0:T(1,128)} %bitcast.4, f32[512,1024]{1,0:T(8,128)} %w_hbm.1, f32[256,512]{1,0:T(8,128)} %wo_hbm.1, ...), custom_call_target="tpu_custom_call" | custom-call | tf_op jit(solution)/shard_map/pallas_call | solution.py:356
  60.1 2.6 %shard_map.112 = (f32[512,1024]{1,0:T(8,128)}, f32[1,512]{1,0:T(1,128)}, f32[256,512]{1,0:T(8,128)}) custom-call(f32[5,512,256]{2,1,0:T(8,128)} %get-tuple-element.10.pieces_ref, f32[1,512]{1,0:T(1,128)} %get-tuple-element.11.table_ref), custom_call_target="tpu_custom_call" | custom-call | tf_op jit(solution)/shard_map/pallas_call | solution.py:427
